TPU v7x, 32 devices: a whole 2x2x4 slice. The times are simulated.
32 devices in a mesh: batch: 8 (over z, y), rows: 4 (over x, core).
Axes of the slice: x: 2, y: 2, z: 4, core: 2. Of those that a mesh axis runs over, the one named last changes fastest.
Arguments:
- frames: bfloat16 [8, 4, 16, 64, 128], P('batch', None, None, 'rows'), may hold values from -6 to 6
- crop_sizes: int32 [8, 2], P('batch'), may hold values from 8 to 128, as said below
- kernel: float32 [1296, 512], P(None, ('batch', 'rows')), may hold values from -0.5 to 0.5
- gate_bias: float32 [512], P(('batch', 'rows')), may hold values from -0.3 to 0.3
- peepholes: float32 [3, 128], P(None, 'batch'), may hold values from -0.6 to 0.6
- cotangent: bfloat16 [8, 4, 64, 128, 128], P('batch', None, 'rows'), may hold values from -6 to 6
- kernel_first: float32 [1296, 512], P(None, ('batch', 'rows')), as said below
- kernel_second: float32 [1296, 512], P(None, ('batch', 'rows')), as said below
- bias_first: float32 [512], P(('batch', 'rows')), as said below
- bias_second: float32 [512], P(('batch', 'rows')), as said below
- peep_first: float32 [3, 128], P(None, 'batch'), as said below
- peep_second: float32 [3, 128], P(None, 'batch'), as said below
Outputs:
- hidden_seq: bfloat16 [8, 4, 64, 128, 128], P('batch', None, 'rows')
- frames_grad: float32 [8, 4, 16, 64, 128], P('batch', None, None, 'rows')
- grad_norm: float32 [], replicated
- kernel_new: float32 [1296, 512], P(None, ('batch', 'rows'))
- kernel_first_new: float32 [1296, 512], P(None, ('batch', 'rows'))
- kernel_second_new: float32 [1296, 512], P(None, ('batch', 'rows'))
- bias_new: float32 [512], P(('batch', 'rows'))
- bias_first_new: float32 [512], P(('batch', 'rows'))
- bias_second_new: float32 [512], P(('batch', 'rows'))
- peep_new: float32 [3, 128], P(None, 'batch')
- peep_first_new: float32 [3, 128], P(None, 'batch')
- peep_second_new: float32 [3, 128], P(None, 'batch')
Inputs may be any that keep to these rules, and one draw needn't show every extreme that they name: `crop_sizes`: column 0 is a crop's height, column 1 its width; in every draw some crop has height 64 and some crop width 128. `kernel_first`: both signs. `kernel_second`: positive. `bias_first`: both signs. `bias_second`: positive. `peep_first`: both signs. `peep_second`: positive.
All inputs are finite; a program needn't handle non-finite values.
Results may differ from a plain program's by a relative error of at most 0.0078.
The roundings to bfloat16 on the way count: a program that leaves them out, or rounds other values in their place, can miss the bound.
Values may be sent and summed in bfloat16 or wider, within the bound.
A program may use at most 192 MiB of HBM per device.

v0:
```python
import jax
import jax.numpy as jnp
from jax import lax
from jax.sharding import PartitionSpec as P

CIN = 16
HID = 128
GATES = 512
KROWS = 1296
ROWS_DEV = 16
ITEMS_DEV = 1
WID = 128
FRAMES = 4
STEP = 5


CLIP_AT = 0.02
LEARN_RATE = 0.02
BETA_ONE = 0.9
BETA_TWO = 0.999
WEIGHT_DECAY = 0.01
ADAM_EPS = 1e-08


def padded(cells, sides, width):
    for axis, dim in sides:
        count = lax.axis_size(axis)
        ends = count - 1
        head = lax.slice_in_dim(cells, 0, width, axis=dim)
        tail = lax.slice_in_dim(cells, cells.shape[dim] - width, cells.shape[dim], axis=dim)
        cells = jnp.concatenate(
            [
                lax.ppermute(tail, axis, [(i, (i + 1) % count) for i in range(ends)]),
                cells,
                lax.ppermute(head, axis, [((i + 1) % count, i) for i in range(ends)]),
            ],
            axis=dim,
        )
    return cells


def adamw_update(weight, gradient, first, second, scale):
    clipped = gradient * scale
    first_new = BETA_ONE * first + (1.0 - BETA_ONE) * clipped
    second_new = BETA_TWO * second + (1.0 - BETA_TWO) * clipped * clipped
    first_hat = first_new / (1.0 - BETA_ONE**STEP)
    second_hat = second_new / (1.0 - BETA_TWO**STEP)
    weight_new = weight - LEARN_RATE * (
        first_hat / (jnp.sqrt(second_hat) + ADAM_EPS) + WEIGHT_DECAY * weight
    )
    return (weight_new, first_new, second_new)


def local(
    frames,
    crop_sizes,
    kernel,
    gate_bias,
    peepholes,
    cotangent,
    kernel_first,
    kernel_second,
    bias_first,
    bias_second,
    peep_first,
    peep_second,
):
    kernel_low = kernel.astype(jnp.bfloat16)
    kernel_part = lax.all_gather(kernel_low, "rows", axis=1, tiled=True)
    kernel_whole = lax.all_gather(kernel_part, "batch", axis=1, tiled=True)
    tap_weights = kernel_whole.reshape(9, CIN + HID, GATES)
    bias_whole = lax.all_gather(gate_bias, ("batch", "rows"), axis=0, tiled=True)
    peep_whole = lax.all_gather(peepholes, "batch", axis=1, tiled=True)
    row_start = lax.axis_index("rows") * ROWS_DEV
    rows_at = row_start + lax.broadcasted_iota(jnp.int32, (ITEMS_DEV, ROWS_DEV, WID), 1)
    cols_at = lax.broadcasted_iota(jnp.int32, (ITEMS_DEV, ROWS_DEV, WID), 2)
    inside = ((rows_at < crop_sizes[:, 0:1, None]) & (cols_at < crop_sizes[:, 1:2, None])).astype(
        jnp.float32
    )
    cell_mask = inside[..., None]
    masked = frames * inside.astype(jnp.bfloat16)[:, None, None]
    framed = padded(masked, (("rows", 3),), 1)
    framed = jnp.transpose(framed, (0, 1, 3, 4, 2))
    framed = jnp.pad(framed, ((0, 0), (0, 0), (0, 0), (1, 1), (0, 0)))
    state_low = jnp.zeros((ITEMS_DEV, ROWS_DEV, WID, HID), jnp.bfloat16)
    cell_state = jnp.zeros((ITEMS_DEV, ROWS_DEV, WID, HID), jnp.float32)
    kept_joined = []
    kept_preact = []
    kept_cells = [cell_state]
    outputs = []
    for frame_index in range(FRAMES):
        if frame_index == 0:
            state_pad = jnp.zeros((ITEMS_DEV, ROWS_DEV + 2, WID + 2, HID), jnp.bfloat16)
        else:
            state_pad = padded(state_low, (("rows", 1),), 1)
            state_pad = jnp.pad(state_pad, ((0, 0), (0, 0), (1, 1), (0, 0)))
        joined = jnp.concatenate([framed[:, frame_index], state_pad], axis=-1)
        summed = jnp.zeros((ITEMS_DEV, ROWS_DEV, WID, GATES), jnp.float32)
        for tap_index in range(9):
            row_shift = tap_index // 3
            col_shift = tap_index % 3
            window = joined[:, row_shift : row_shift + ROWS_DEV, col_shift : col_shift + WID]
            summed = summed + jnp.einsum(
                "nhwc,cg->nhwg", window, tap_weights[tap_index], preferred_element_type=jnp.float32
            )
        preact = summed + bias_whole
        in_gate = jax.nn.sigmoid(preact[..., :HID] + peep_whole[0] * cell_state)
        forget = jax.nn.sigmoid(preact[..., HID : 2 * HID] + peep_whole[1] * cell_state)
        candidate = jnp.tanh(preact[..., 2 * HID : 3 * HID])
        cell_next = cell_mask * (forget * cell_state + in_gate * candidate)
        out_gate = jax.nn.sigmoid(preact[..., 3 * HID :] + peep_whole[2] * cell_next)
        state_low = (cell_mask * out_gate * jnp.tanh(cell_next)).astype(jnp.bfloat16)
        kept_joined.append(joined)
        kept_preact.append(preact)
        kept_cells.append(cell_next)
        outputs.append(state_low)
        cell_state = cell_next
    hidden_seq = jnp.stack(outputs, axis=1)
    grad_state = jnp.zeros((ITEMS_DEV, ROWS_DEV, WID, HID), jnp.float32)
    grad_cell = jnp.zeros((ITEMS_DEV, ROWS_DEV, WID, HID), jnp.float32)
    tap_acc = [jnp.zeros((CIN + HID, GATES), jnp.float32) for tap_index in range(9)]
    bias_acc = jnp.zeros((GATES,), jnp.float32)
    peep_acc = jnp.zeros((3, HID), jnp.float32)
    frame_pads = [None] * FRAMES
    for frame_index in reversed(range(FRAMES)):
        preact = kept_preact[frame_index]
        cell_prev = kept_cells[frame_index]
        cell_next = kept_cells[frame_index + 1]
        joined = kept_joined[frame_index]
        in_gate = jax.nn.sigmoid(preact[..., :HID] + peep_whole[0] * cell_prev)
        forget = jax.nn.sigmoid(preact[..., HID : 2 * HID] + peep_whole[1] * cell_prev)
        candidate = jnp.tanh(preact[..., 2 * HID : 3 * HID])
        out_gate = jax.nn.sigmoid(preact[..., 3 * HID :] + peep_whole[2] * cell_next)
        squashed = jnp.tanh(cell_next)
        total = cell_mask * (cotangent[:, frame_index].astype(jnp.float32) + grad_state)
        grad_out = total * squashed * out_gate * (1.0 - out_gate)
        grad_next = (
            total * out_gate * (1.0 - squashed * squashed) + grad_cell + peep_whole[2] * grad_out
        )
        kept_grad = cell_mask * grad_next
        grad_in = kept_grad * candidate * in_gate * (1.0 - in_gate)
        grad_forget = kept_grad * cell_prev * forget * (1.0 - forget)
        grad_cand = kept_grad * in_gate * (1.0 - candidate * candidate)
        grad_cell = kept_grad * forget + peep_whole[0] * grad_in + peep_whole[1] * grad_forget
        peep_acc = peep_acc + jnp.stack(
            [
                jnp.sum(grad_in * cell_prev, axis=(0, 1, 2)),
                jnp.sum(grad_forget * cell_prev, axis=(0, 1, 2)),
                jnp.sum(grad_out * cell_next, axis=(0, 1, 2)),
            ]
        )
        grad_pre = jnp.concatenate([grad_in, grad_forget, grad_cand, grad_out], axis=-1)
        bias_acc = bias_acc + jnp.sum(grad_pre, axis=(0, 1, 2))
        grad_low = grad_pre.astype(jnp.bfloat16)
        grad_padded = jnp.pad(grad_low, ((0, 0), (2, 2), (2, 2), (0, 0)))
        joint_back = jnp.zeros((ITEMS_DEV, ROWS_DEV + 2, WID + 2, CIN + HID), jnp.float32)
        for tap_index in range(9):
            row_shift = tap_index // 3
            col_shift = tap_index % 3
            window = joined[:, row_shift : row_shift + ROWS_DEV, col_shift : col_shift + WID]
            tap_acc[tap_index] = tap_acc[tap_index] + jnp.einsum(
                "nhwc,nhwg->cg", window, grad_low, preferred_element_type=jnp.float32
            )
            back_window = grad_padded[
                :, 2 - row_shift : 4 - row_shift + ROWS_DEV, 2 - col_shift : 4 - col_shift + WID
            ]
            joint_back = joint_back + jnp.einsum(
                "nhwg,cg->nhwc",
                back_window,
                tap_weights[tap_index],
                preferred_element_type=jnp.float32,
            )
        frame_pads[frame_index] = joint_back[..., :CIN]
        if frame_index > 0:
            state_back = joint_back[..., CIN:]
            rim_rows = jnp.concatenate([state_back[:, 0:1, 1:-1], state_back[:, -1:, 1:-1]], axis=1)
            received = padded(rim_rows.astype(jnp.bfloat16), (("rows", 1),), 1).astype(
                rim_rows.dtype
            )
            grad_state = state_back[:, 1:-1, 1:-1]
            grad_state = grad_state.at[:, 0].add(received[:, 0]).at[:, -1].add(received[:, 3])
    frame_stack = jnp.stack(frame_pads, axis=1)
    rim_rows = jnp.concatenate([frame_stack[:, :, 0:1, 1:-1], frame_stack[:, :, -1:, 1:-1]], axis=2)
    received = padded(rim_rows.astype(jnp.bfloat16), (("rows", 2),), 1).astype(rim_rows.dtype)
    center = frame_stack[:, :, 1:-1, 1:-1]
    center = center.at[:, :, 0].add(received[:, :, 0]).at[:, :, -1].add(received[:, :, 3])
    frames_grad = jnp.transpose(center, (0, 1, 4, 2, 3)) * inside[:, None, None]
    kernel_local = jnp.stack(tap_acc).reshape(KROWS, GATES)
    bias_local = bias_acc[None]
    kernel_half, bias_half = (
        lax.psum_scatter(kernel_local, "batch", scatter_dimension=1, tiled=True),
        lax.psum_scatter(bias_local, "batch", scatter_dimension=1, tiled=True),
    )
    kernel_grad, bias_grad = (
        lax.psum_scatter(kernel_half, "rows", scatter_dimension=1, tiled=True),
        lax.psum_scatter(bias_half, "rows", scatter_dimension=1, tiled=True),
    )
    bias_grad = bias_grad[0]
    peep_total = lax.psum(peep_acc, ("batch", "rows"))
    peep_width = peepholes.shape[1]
    peep_grad = lax.dynamic_slice_in_dim(
        peep_total, lax.axis_index("batch") * peep_width, peep_width, 1
    )
    owned_squares = jnp.sum(kernel_grad * kernel_grad) + jnp.sum(bias_grad * bias_grad)
    squares = lax.psum(owned_squares, ("batch", "rows")) + jnp.sum(peep_total * peep_total)
    grad_norm = jnp.sqrt(squares)
    scale = jnp.minimum(1.0, CLIP_AT / (grad_norm + 1e-06))
    kernel_new, kernel_first_new, kernel_second_new = adamw_update(
        kernel, kernel_grad, kernel_first, kernel_second, scale
    )
    bias_new, bias_first_new, bias_second_new = adamw_update(
        gate_bias, bias_grad, bias_first, bias_second, scale
    )
    peep_new, peep_first_new, peep_second_new = adamw_update(
        peepholes, peep_grad, peep_first, peep_second, scale
    )
    return (
        hidden_seq,
        frames_grad,
        grad_norm,
        kernel_new,
        kernel_first_new,
        kernel_second_new,
        bias_new,
        bias_first_new,
        bias_second_new,
        peep_new,
        peep_first_new,
        peep_second_new,
    )


def solution(mesh):
    return jax.shard_map(
        local,
        mesh=mesh,
        in_specs=(
            P("batch", None, None, "rows", None),
            P("batch", None),
            P(None, ("batch", "rows")),
            P(("batch", "rows")),
            P(None, "batch"),
            P("batch", None, "rows", None, None),
            P(None, ("batch", "rows")),
            P(None, ("batch", "rows")),
            P(("batch", "rows")),
            P(("batch", "rows")),
            P(None, "batch"),
            P(None, "batch"),
        ),
        out_specs=(
            P("batch", None, "rows", None, None),
            P("batch", None, None, "rows", None),
            P(),
            P(None, ("batch", "rows")),
            P(None, ("batch", "rows")),
            P(None, ("batch", "rows")),
            P(("batch", "rows")),
            P(("batch", "rows")),
            P(("batch", "rows")),
            P(None, "batch"),
            P(None, "batch"),
            P(None, "batch"),
        ),
        check_vma=False,
    )
```

profile of v0, /device:TPU:0, one launch (start us, length us, event | category | flops | bytes accessed | tf_op | source)
XLA Modules:
  0.0 660.3 jit_solution(14878436890642993544)
XLA Ops:
  8.1 7.2 %all_gather.12 = bf16[1296,64]{0,1:T(8,128)(2,1)} all-gather(bf16[1296,16]{0,1:T(8,128)(2,1)S(1)} %convert_element_type.298), channel_id=1, replica_groups=mesh['batch'=8,'rows'=4] {'rows'}, dimensions={1}, use_global_device_ids=true | all-gather | bytes 207360 | tf_op jit(solution)/shard_map/all_gather | solution.py:69
  22.7 26.9 %all-gather = f32[8,16,3]{1,2,0:T(4,128)S(1)} all-gather(f32[1,16,3]{1,2,0:T(4,128)} %bitcast.794), channel_id=1, replica_groups=mesh['batch'=8,'rows'=4] {'batch'}, dimensions={0}, use_global_device_ids=true | all-gather | bytes 1728 | tf_op jit(solution)/shard_map/all_gather | solution.py:73
  50.5 40.7 %all-reduce.9 = f32[512]{0:T(512)S(1)} all-reduce(f32[512]{0:T(512)S(1)} %dynamic-update-slice.24), channel_id=1, replica_groups=mesh['batch'=8,'rows'=4] {'batch','rows'}, use_global_device_ids=true, to_apply=%add.9 | all-reduce | flops 512 | bytes 4096
  95.5 2.8 fusion.310
  98.3 3.0 fusion.307
  101.4 3.2 fusion.304
  104.6 2.9 fusion.301
  107.4 3.1 fusion.298
  110.5 2.8 fusion.319
  113.3 9.6 %add_bitcast_fusion.3 = f32[1,16,128,512]{3,2,1,0:T(8,128)S(1)} fusion(f32[16,128,512]{2,1,0:T(8,128)} %fusion.298, f32[16,128,512]{2,1,0:T(8,128)} %fusion.301, f32[16,128,512]{2,1,0:T(8,128)} %fusion.304, f32[16,128,512]{2,1,0:T(8,128)} %fusion.307, f32[16,128,512]{2,1,0:T(8,128)} %fusion.310, f32[16,128,512]{2,1,0:T(8,128)S(1)} %fusion.313, ...), kind=kOutput, calls=%fused_computation.16 | convolution fusion | flops 311427072 | bytes 38160384 | tf_op jit(solution)/shard_map/nhwc,cg->nhwg/dot_general | solution.py:103
  129.7 3.1 collective-permute-done.3
  137.5 2.9 fusion.416
  140.4 2.9 fusion.413
  143.2 2.8 fusion.410
  148.8 2.9 fusion.404
  151.7 2.8 fusion.425
  154.6 10.6 %add_bitcast_fusion.2 = f32[1,16,128,512]{3,2,1,0:T(8,128)S(1)} fusion(f32[16,128,512]{2,1,0:T(8,128)} %fusion.425, f32[16,128,512]{2,1,0:T(8,128)} %fusion.404, f32[16,128,512]{2,1,0:T(8,128)} %fusion.407, f32[16,128,512]{2,1,0:T(8,128)} %fusion.410, f32[16,128,512]{2,1,0:T(8,128)} %fusion.413, f32[16,128,512]{2,1,0:T(8,128)} %fusion.416, ...), kind=kOutput, calls=%fused_computation.15 | convolution fusion | flops 312606720 | bytes 39266304 | tf_op jit(solution)/shard_map/nhwc,cg->nhwg/dot_general | solution.py:103
  167.5 4.6 collective-permute-start.4
  177.2 2.9 fusion.443
  182.9 2.9 fusion.437
  185.8 2.8 fusion.434
  188.6 2.8 fusion.431
  194.2 2.9 fusion.449
  197.1 10.6 %add_bitcast_fusion.1 = f32[1,16,128,512]{3,2,1,0:T(8,128)S(1)} fusion(f32[16,128,512]{2,1,0:T(8,128)} %fusion.449, f32[16,128,512]{2,1,0:T(8,128)} %fusion.428, f32[16,128,512]{2,1,0:T(8,128)} %fusion.431, f32[16,128,512]{2,1,0:T(8,128)} %fusion.434, f32[16,128,512]{2,1,0:T(8,128)} %fusion.437, f32[16,128,512]{2,1,0:T(8,128)} %fusion.440, ...), kind=kOutput, calls=%fused_computation.14 | convolution fusion | flops 312606720 | bytes 39266304 | tf_op jit(solution)/shard_map/nhwc,cg->nhwg/dot_general | solution.py:103
  211.5 4.1 collective-permute-start.6
  221.1 2.8 fusion.467
  223.9 2.9 fusion.464
  229.5 2.9 fusion.458
  232.4 2.9 fusion.455
  235.3 2.8 fusion.452
  238.1 2.8 fusion.473
  240.8 10.7 %add_bitcast_fusion = f32[1,16,128,512]{3,2,1,0:T(8,128)S(1)} fusion(f32[16,128,512]{2,1,0:T(8,128)} %fusion.473, f32[16,128,512]{2,1,0:T(8,128)} %fusion.452, f32[16,128,512]{2,1,0:T(8,128)} %fusion.455, f32[16,128,512]{2,1,0:T(8,128)} %fusion.458, f32[16,128,512]{2,1,0:T(8,128)} %fusion.461, f32[16,128,512]{2,1,0:T(8,128)} %fusion.464, ...), kind=kOutput, calls=%fused_computation.13 | convolution fusion | flops 312606720 | bytes 39266304 | tf_op jit(solution)/shard_map/nhwc,cg->nhwg/dot_general | solution.py:103
  251.6 2.9 multiply_reduce_fusion.9
  278.9 8.5 %add_bitcast_fusion.7 = f32[1,18,130,144]{3,2,1,0:T(8,128)S(1)} fusion(f32[18,130,144]{2,1,0:T(8,128)} %fusion.22, f32[18,130,144]{2,1,0:T(8,128)} %fusion.19, f32[18,130,144]{2,1,0:T(8,128)} %fusion.16, f32[18,130,144]{2,1,0:T(8,128)} %fusion.13, f32[18,130,144]{2,1,0:T(8,128)} %fusion.10, f32[18,130,144]{2,1,0:T(8,128)} %fusion.7, ...), kind=kOutput, calls=%fused_computation.128 | convolution fusion | flops 347742720 | bytes 14489856 | tf_op jit(solution)/shard_map/nhwg,cg->nhwc/dot_general | solution.py:167
  287.5 4.0 collective-permute-start.8
  334.3 8.5 %add_bitcast_fusion.6 = f32[1,18,130,144]{3,2,1,0:T(8,128)S(1)} fusion(f32[18,130,144]{2,1,0:T(8,128)} %fusion.49, f32[18,130,144]{2,1,0:T(8,128)} %fusion.46, f32[18,130,144]{2,1,0:T(8,128)} %fusion.43, f32[18,130,144]{2,1,0:T(8,128)} %fusion.40, f32[18,130,144]{2,1,0:T(8,128)} %fusion.37, f32[18,130,144]{2,1,0:T(8,128)} %fusion.34, ...), kind=kOutput, calls=%fused_computation.127 | convolution fusion | flops 347742720 | bytes 14489856 | tf_op jit(solution)/shard_map/nhwg,cg->nhwc/dot_general | solution.py:167
  343.0 4.1 collective-permute-start.10
  386.5 6.6 %add_bitcast_fusion.5 = f32[1,18,130,144]{3,2,1,0:T(8,128)S(1)} fusion(f32[18,130,144]{2,1,0:T(8,128)} %fusion.76, f32[18,130,144]{2,1,0:T(8,128)} %fusion.73, f32[18,130,144]{2,1,0:T(8,128)} %fusion.70, f32[18,130,144]{2,1,0:T(8,128)} %fusion.67, f32[18,130,144]{2,1,0:T(8,128)S(1)} %fusion.64, f32[18,130,144]{2,1,0:T(8,128)S(1)} %fusion.61, ...), kind=kOutput, calls=%fused_computation.126 | convolution fusion | flops 347742720 | bytes 17966592 | tf_op jit(solution)/shard_map/nhwg,cg->nhwc/dot_general | solution.py:167
  393.3 4.0 collective-permute-start.12
  398.7 2.8 fusion.155
  424.8 3.0 fusion.127
  436.4 49.3 %reduce-scatter.13.cloned.1.call-done = f32[64,1]{1,0:T(8,128)} async-done(((f32[512,1]{1,0:T(8,128)}), f32[64,1]{1,0:T(8,128)}) %reduce-scatter.13.cloned.1.call-update) | async-done | bytes 272
  485.8 2.9 fusion.151
  488.7 3.3 copy.229
  497.4 3.2 pad_maximum_fusion.4
  525.7 56.3 %reduce-scatter.9.cloned.1.call-done = f32[1296,64]{0,1:T(8,128)} async-done(((f32[1296,512]{0,1:T(8,128)}), f32[1296,64]{0,1:T(8,128)}) %reduce-scatter.9.cloned.1.call-update) | async-done | bytes 331792 | tf_op jit(solution)/shard_map/reduce_scatter | solution.py:191
  582.8 21.5 %reduce-scatter.11.cloned.1.call-done = f32[1296,16]{0,1:T(8,128)} async-done(((f32[1296,64]{0,1:T(8,128)}), f32[1296,16]{0,1:T(8,128)}) %reduce-scatter.11.cloned.1.call-update) | async-done | bytes 82960 | tf_op jit(solution)/shard_map/reduce_scatter | solution.py:195
  608.1 39.3 %all-reduce.10 = (f32[]{:T(128)}, f32[3,128]{1,0:T(4,128)S(1)}) all-reduce(f32[]{:T(128)S(6)} %add.892, f32[3,128]{1,0:T(4,128)S(1)} %fusion.340), channel_id=1, replica_groups=mesh['batch'=8,'rows'=4] {'batch','rows'}, use_global_device_ids=true, to_apply=%region_10.11 | all-reduce | flops 385 | bytes 3080 | tf_op jit(solution)/shard_map/psum | solution.py:205
  (375 shorter events, 229.1 us)
Async XLA Ops:
  7.2 85.0 %all-gather.3.cloned.1.call-start = ((), (), s32[]{:S(2)}) async-start(), calls=%async_computation.4 | async-start | bytes 1622016 | tf_op jit(solution)/shard_map/all_gather | solution.py:70
  15.3 470.4 %reduce-scatter.13.cloned.1.call-start = ((), (), s32[]{:S(2)}) async-start(), calls=%async_computation.7 | async-start | bytes 294912
  19.1 72.1 %collective-permute-start = (bf16[1,4,16,1,128]{4,2,3,1,0:T(8,128)(2,1)S(1)}, bf16[1,4,16,1,128]{4,2,3,1,0:T(8,128)(2,1)S(1)}, u32[]{:S(2)}, u32[]{:S(2)}) collective-permute-start(bf16[1,4,16,1,128]{4,2,3,1,0:T(8,128)(2,1)S(1)} %get-tuple-element.235), channel_id=1, source_target_pairs={{0,1},{1,2},{2,3},{4,5},{5,6},{6,7},{8,9},{9,10},{10,11},{12,13},{... | collective-permute-start | bytes 49160 | tf_op jit(solution)/shard_map/ppermute | solution.py:33
  21.4 69.9 %collective-permute-start.1 = (bf16[1,4,16,1,128]{4,2,3,1,0:T(8,128)(2,1)S(1)}, bf16[1,4,16,1,128]{4,2,3,1,0:T(8,128)(2,1)S(1)}, u32[]{:S(2)}, u32[]{:S(2)}) collective-permute-start(bf16[1,4,16,1,128]{4,2,3,1,0:T(8,128)(2,1)S(1)} %get-tuple-element.236), channel_id=1, source_target_pairs={{1,0},{2,1},{3,2},{5,4},{6,5},{7,6},{9,8},{10,9},{11,10},{13,12},{... | collective-permute-start | bytes 49160 | tf_op jit(solution)/shard_map/ppermute | solution.py:35
  49.6 73.3 %copy-start.43 = (f32[128]{0:T(128)}, f32[128]{0:T(128)S(1)}, u32[]{:S(2)}) copy-start(f32[128]{0:T(128)S(1)} %get-tuple-element.239) | copy-start | bytes 1540
  49.6 73.3 %copy-start.47 = (f32[128]{0:T(128)}, f32[128]{0:T(128)S(1)}, u32[]{:S(2)}) copy-start(f32[128]{0:T(128)S(1)} %get-tuple-element.240) | copy-start | bytes 1540
  49.6 303.6 %copy-start.41 = (f32[128]{0:T(128)}, f32[128]{0:T(128)S(1)}, u32[]{:S(2)}) copy-start(f32[128]{0:T(128)S(1)} %get-tuple-element.237) | copy-start | bytes 1540
  92.2 21.1 %copy-start.17 = (bf16[1,18,130,16]{2,3,1,0:T(8,128)(2,1)}, bf16[1,18,130,16]{2,3,1,0:T(8,128)(2,1)S(1)}, u32[]{:S(2)}) copy-start(bf16[1,18,130,16]{2,3,1,0:T(8,128)(2,1)S(1)} %get-tuple-element.231) | copy-start | bytes 224644
  124.9 40.3 %copy-start.11 = (f32[1,16,128,128]{3,2,1,0:T(8,128)}, f32[1,16,128,128]{3,2,1,0:T(8,128)S(1)}, u32[]{:S(2)}) copy-start(f32[1,16,128,128]{3,2,1,0:T(8,128)S(1)} %get-tuple-element.203) | copy-start | bytes 3145732
  125.6 4.0 collective-permute-start.2
  126.9 5.8 collective-permute-start.3
  129.6 24.9 %copy-start.5 = (bf16[1,18,130,16]{3,2,1,0:T(8,128)(2,1)}, bf16[1,18,130,16]{3,2,1,0:T(8,128)(2,1)S(1)}, u32[]{:S(2)}) copy-start(bf16[1,18,130,16]{3,2,1,0:T(8,128)(2,1)S(1)} %copy.166) | copy-start | bytes 224644
  134.0 20.6 %copy-start.7 = (bf16[1,18,130,128]{3,2,1,0:T(8,128)(2,1)}, bf16[1,18,130,128]{3,2,1,0:T(8,128)(2,1)S(1)}, u32[]{:S(2)}) copy-start(bf16[1,18,130,128]{3,2,1,0:T(8,128)(2,1)S(1)} %select_maximum_fusion.4) | copy-start | bytes 1797124
  167.5 6.6 %collective-permute-start.4 = (bf16[1,1,128,128]{3,2,1,0:T(8,128)(2,1)S(1)}, bf16[1,1,128,128]{3,2,1,0:T(8,128)(2,1)S(1)}, u32[]{:S(2)}, u32[]{:S(2)}) collective-permute-start(bf16[1,1,128,128]{3,2,1,0:T(8,128)(2,1)S(1)} %get-tuple-element.227), channel_id=1, source_target_pairs={{0,1},{1,2},{2,3},{4,5},{5,6},{6,7},{8,9},{9,10},{10,11},{12,13},{... | collective-permute-start | bytes 98312 | tf_op jit(solution)/shard_map/ppermute | solution.py:33
  172.1 3.1 collective-permute-start.5
  197.1 10.6 %copy-start.14 = (f32[1,16,128,128]{3,2,1,0:T(8,128)S(1)}, f32[1,16,128,128]{3,2,1,0:T(8,128)}, u32[]{:S(2)}) copy-start(f32[1,16,128,128]{3,2,1,0:T(8,128)} %get-tuple-element.201) | copy-start | bytes 3145732
  211.5 6.0 collective-permute-start.6
  215.6 3.4 collective-permute-start.7
  240.8 10.7 %copy-start.13 = (f32[1,16,128,128]{3,2,1,0:T(8,128)S(1)}, f32[1,16,128,128]{3,2,1,0:T(8,128)}, u32[]{:S(2)}) copy-start(f32[1,16,128,128]{3,2,1,0:T(8,128)} %get-tuple-element.199) | copy-start | bytes 3145732
  278.9 15.9 %copy-start.4 = (f32[1,16,128,512]{3,2,1,0:T(8,128)S(1)}, f32[1,16,128,512]{3,2,1,0:T(8,128)}, u32[]{:S(2)}) copy-start(f32[1,16,128,512]{3,2,1,0:T(8,128)} %copy-done.3) | copy-start | bytes 12582916
  287.4 8.7 %copy-start.19 = (f32[1,18,130,144]{3,2,1,0:T(8,128)}, f32[1,18,130,144]{3,2,1,0:T(8,128)S(1)}, u32[]{:S(2)}) copy-start(f32[1,18,130,144]{3,2,1,0:T(8,128)S(1)} %add_bitcast_fusion.7) | copy-start | bytes 4043524
  287.5 5.7 collective-permute-start.8
  291.5 3.1 collective-permute-start.9
  334.3 15.9 %copy-start.2 = (f32[1,16,128,512]{3,2,1,0:T(8,128)S(1)}, f32[1,16,128,512]{3,2,1,0:T(8,128)}, u32[]{:S(2)}) copy-start(f32[1,16,128,512]{3,2,1,0:T(8,128)} %copy-done.1) | copy-start | bytes 12582916
  342.9 8.8 %copy-start.20 = (f32[1,18,130,144]{3,2,1,0:T(8,128)}, f32[1,18,130,144]{3,2,1,0:T(8,128)S(1)}, u32[]{:S(2)}) copy-start(f32[1,18,130,144]{3,2,1,0:T(8,128)S(1)} %add_bitcast_fusion.6) | copy-start | bytes 4043524
  343.0 5.7 collective-permute-start.10
  347.0 3.1 collective-permute-start.11
  386.5 12.1 %copy-start.31 = (bf16[16,128,128]{2,1,0:T(8,128)(2,1)S(1)}, bf16[16,128,128]{2,1,0:T(8,128)(2,1)}, u32[]{:S(2)}) copy-start(bf16[16,128,128]{2,1,0:T(8,128)(2,1)} %get-tuple-element.222) | copy-start | bytes 1572868
  386.5 12.1 %copy-start.32 = (bf16[16,128,128]{2,1,0:T(8,128)(2,1)S(1)}, bf16[16,128,128]{2,1,0:T(8,128)(2,1)}, u32[]{:S(2)}) copy-start(bf16[16,128,128]{2,1,0:T(8,128)(2,1)} %get-tuple-element.180) | copy-start | bytes 1572868
  386.5 12.2 %copy-start.33 = (bf16[16,128,128]{2,1,0:T(8,128)(2,1)S(1)}, bf16[16,128,128]{2,1,0:T(8,128)(2,1)}, u32[]{:S(2)}) copy-start(bf16[16,128,128]{2,1,0:T(8,128)(2,1)} %get-tuple-element.208) | copy-start | bytes 1572868
  386.5 12.2 %copy-start.80 = (f32[144,512]{1,0:T(8,128)S(1)}, f32[144,512]{1,0:T(8,128)}, u32[]{:S(2)}) copy-start(f32[144,512]{1,0:T(8,128)} %convolution_bitcast_fusion.31) | copy-start | bytes 884740
  393.2 22.8 %copy-start.22 = (f32[1,18,130,144]{3,2,1,0:T(8,128)}, f32[1,18,130,144]{3,2,1,0:T(8,128)S(1)}, u32[]{:S(2)}) copy-start(f32[1,18,130,144]{3,2,1,0:T(8,128)S(1)} %add_bitcast_fusion.5) | copy-start | bytes 4043524
  393.3 22.7 %collective-permute-start.12 = (bf16[1,1,128,128]{3,2,1,0:T(8,128)(2,1)S(1)}, bf16[1,1,128,128]{3,2,1,0:T(8,128)(2,1)S(1)}, u32[]{:S(2)}, u32[]{:S(2)}) collective-permute-start(bf16[1,1,128,128]{3,2,1,0:T(8,128)(2,1)S(1)} %get-tuple-element.213), channel_id=1, source_target_pairs={{0,1},{1,2},{2,3},{4,5},{5,6},{6,7},{8,9},{9,10},{10,11},{12,13},{... | collective-permute-start | bytes 98312 | tf_op jit(solution)/shard_map/ppermute | solution.py:33
  397.4 18.7 %collective-permute-start.13 = (bf16[1,1,128,128]{3,2,1,0:T(8,128)(2,1)S(1)}, bf16[1,1,128,128]{3,2,1,0:T(8,128)(2,1)S(1)}, u32[]{:S(2)}, u32[]{:S(2)}) collective-permute-start(bf16[1,1,128,128]{3,2,1,0:T(8,128)(2,1)S(1)} %get-tuple-element.214), channel_id=1, source_target_pairs={{1,0},{2,1},{3,2},{5,4},{6,5},{7,6},{9,8},{10,9},{11,10},{13,12},{... | collective-permute-start | bytes 98312 | tf_op jit(solution)/shard_map/ppermute | solution.py:35
  424.7 100.3 %reduce-scatter.15.cloned.1.call-start = ((), (), s32[]{:S(2)}) async-start(), calls=%async_computation.8 | async-start | bytes 40960
  485.8 96.3 %reduce-scatter.9.cloned.1.call-start = ((), (), s32[]{:S(2)}) async-start(), calls=%async_computation.5 | async-start | bytes 3244032 | tf_op jit(solution)/shard_map/reduce_scatter | solution.py:191
  492.0 112.3 %reduce-scatter.11.cloned.1.call-start = ((), (), s32[]{:S(2)}) async-start(), calls=%async_computation.6 | async-start | bytes 450560 | tf_op jit(solution)/shard_map/reduce_scatter | solution.py:195
  521.8 60.9 %collective-permute-start.14 = (bf16[1,4,1,128,16]{3,4,2,1,0:T(8,128)(2,1)S(1)}, bf16[1,4,1,128,16]{3,4,2,1,0:T(8,128)(2,1)S(1)}, u32[]{:S(2)}, u32[]{:S(2)}) collective-permute-start(bf16[1,4,1,128,16]{3,4,2,1,0:T(8,128)(2,1)S(1)} %get-tuple-element.219), channel_id=1, source_target_pairs={{0,1},{1,2},{2,3},{4,5},{5,6},{6,7},{8,9},{9,10},{10,11},{12,13},{... | collective-permute-start | bytes 49160 | tf_op jit(solution)/shard_map/ppermute | solution.py:33
  523.0 59.6 %collective-permute-start.15 = (bf16[1,4,1,128,16]{3,4,2,1,0:T(8,128)(2,1)S(1)}, bf16[1,4,1,128,16]{3,4,2,1,0:T(8,128)(2,1)S(1)}, u32[]{:S(2)}, u32[]{:S(2)}) collective-permute-start(bf16[1,4,1,128,16]{3,4,2,1,0:T(8,128)(2,1)S(1)} %get-tuple-element.220), channel_id=1, source_target_pairs={{1,0},{2,1},{3,2},{5,4},{6,5},{7,6},{9,8},{10,9},{11,10},{13,12},{... | collective-permute-start | bytes 49160 | tf_op jit(solution)/shard_map/ppermute | solution.py:35
  524.7 124.7 %copy-start.62 = (f32[16]{0:T(128)S(1)}, f32[16]{0:T(128)}, u32[]{:S(2)}) copy-start(f32[16]{0:T(128)} %param.31) | copy-start | bytes 196
  524.7 124.7 %copy-start.63 = (f32[16]{0:T(128)S(1)}, f32[16]{0:T(128)}, u32[]{:S(2)}) copy-start(f32[16]{0:T(128)} %param.36) | copy-start | bytes 196
  524.7 124.7 %copy-start.64 = (f32[16]{0:T(128)S(1)}, f32[16]{0:T(128)}, u32[]{:S(2)}) copy-start(f32[16]{0:T(128)} %param.37) | copy-start | bytes 196
  524.7 125.3 %copy-start.46 = (f32[3,16]{1,0:T(4,128)S(1)}, f32[3,16]{1,0:T(4,128)}, u32[]{:S(2)}) copy-start(f32[3,16]{1,0:T(4,128)} %param.32) | copy-start | bytes 580
  524.7 125.3 %copy-start.60 = (f32[3,16]{1,0:T(4,128)S(1)}, f32[3,16]{1,0:T(4,128)}, u32[]{:S(2)}) copy-start(f32[3,16]{1,0:T(4,128)} %param.38) | copy-start | bytes 580
  524.7 125.2 %copy-start.61 = (f32[3,16]{1,0:T(4,128)S(1)}, f32[3,16]{1,0:T(4,128)}, u32[]{:S(2)}) copy-start(f32[3,16]{1,0:T(4,128)} %param.39) | copy-start | bytes 580
  524.8 125.9 %copy-start.38 = (f32[1296,16]{0,1:T(8,128)S(1)}, f32[1296,16]{0,1:T(8,128)}, u32[]{:S(2)}) copy-start(f32[1296,16]{0,1:T(8,128)} %param.30) | copy-start | bytes 248836
  524.8 125.9 %copy-start.39 = (f32[1296,16]{0,1:T(8,128)S(1)}, f32[1296,16]{0,1:T(8,128)}, u32[]{:S(2)}) copy-start(f32[1296,16]{0,1:T(8,128)} %param.34) | copy-start | bytes 248836
  524.8 125.9 %copy-start.40 = (f32[1296,16]{0,1:T(8,128)S(1)}, f32[1296,16]{0,1:T(8,128)}, u32[]{:S(2)}) copy-start(f32[1296,16]{0,1:T(8,128)} %param.35) | copy-start | bytes 248836
  (61 other events, 133.9 us)
Sparse Core Ops, SparseCore 0:
  15.4 44.8 all-gather.2
  424.8 60.8 reduce-scatter.12
  488.2 18.3 reduce-scatter.14
  510.4 71.5 reduce-scatter.8
  584.5 19.7 reduce-scatter.10
where the time goes:
time: 669 us; the launch traced here: 660 us
  matrix products  273 us (41%)
  waiting for transfers between devices  136 us (20%)
  blocking collectives  114 us (17%)
  other arithmetic  48.9 us (7%)
  starting transfers between devices  37.2 us (6%)
  local copies, waits for them, and re-layouts  32.1 us (5%)
  between operations  19.4 us (3%)
    dot_general x36, matrix products, local(): jnp.einsum('nhwc,cg->nhwg', window, tap_weights[tap_index], preferred_ele...  124 us
    dot_general x36, matrix products, local(): jnp.einsum('nhwg,cg->nhwc', back_window, tap_weights[tap_index], preferre...  86.3 us
    dot_general x36, matrix products, local(): jnp.einsum('nhwc,nhwg->cg', window, grad_low, preferred_element_type=jnp....  62 us
    reduce_scatter x1, waiting for transfers between devices, local(): lax.psum_scatter(kernel_local, 'batch', scatter_dimension=1, tiled=True)  56.3 us
    unnamed x7, waiting for transfers between devices  49.5 us
    unnamed x1, blocking collectives  40.7 us
    psum x1, blocking collectives, local(): lax.psum(owned_squares, ('batch', 'rows'))  39.3 us
    all_gather x1, blocking collectives, local(): peep_whole = lax.all_gather(peepholes, 'batch', axis=1, tiled=True)  26.9 us
  transfers between devices with their start and end apart: 21, of which 8 were waited for; matrix products, arithmetic and copies ran while one was open for 11% of the time, Pallas kernels for 0%

commit v1 on v0

v1 whole, which is shorter than its diff:
```python
import functools
import math

import jax
import jax.numpy as jnp
from jax import lax
from jax.experimental import pallas as pl
from jax.experimental.pallas import tpu as pltpu
from jax.sharding import PartitionSpec as P

CIN = 16
HID = 128
GATES = 512
KROWS = 1296
WID = 128
STEP = 5
CLIP_AT = 0.02
LEARN_RATE = 0.02
BETA_ONE = 0.9
BETA_TWO = 0.999
WEIGHT_DECAY = 0.01
ADAM_EPS = 1e-08

F32 = jnp.float32
BF16 = jnp.bfloat16
MESH = pl.DeviceIdType.MESH
NT = (((1,), (1,)), ((), ()))
NN = (((1,), (0,)), ((), ()))

WIDE = 3 * HID
HALL = 3 * WIDE
FEAT = 3 * CIN
FPAD = 256
KALL = HALL + FPAD
SUB = 32
UNIT = 16


def sigmoid(v):
    return 0.5 * jnp.tanh(0.5 * v) + 0.5


def mm(a, b, dims):
    return lax.dot_general(a, b, dims, preferred_element_type=F32)


def layer_kernel(
    dims,
    crop_ref,
    frames_ref,
    kt_ref,
    small_ref,
    cot_hbm,
    hid_hbm,
    fg_ref,
    grad_ref,
    small_out,
    norm_out,
    wt,
    wft,
    fr,
    xt,
    sc,
    gates,
    cells,
    gpre,
    gcell,
    gs,
    ybuf,
    fgb,
    cot,
    hlast,
    srow,
    consts,
    sums,
    acc,
    facc,
    fhalo_s,
    fhalo_r,
    shalo_r,
    ghalo_s,
    ghalo_r,
    bhalo_s,
    bhalo_r,
    nat,
    sm1,
    sm2,
    *rest,
):
    nbat, nrow, frames_n, rows_n, hi_bits, lo_bits = dims
    pix = rows_n * WID
    rest = list(rest)
    stage_send = [rest.pop(0) for _ in range(4 * hi_bits)]
    stage_recv = [rest.pop(0) for _ in range(4 * hi_bits)]
    last_send = [rest.pop(0) for _ in range(4)]
    last_recv = [rest.pop(0) for _ in range(4)]
    lo_send = [rest.pop(0) for _ in range(lo_bits)]
    lo_recv = [rest.pop(0) for _ in range(2 * lo_bits)]
    sems = rest.pop(0)
    rsems = rest.pop(0)
    lsems = rest.pop(0)

    at_b = lax.axis_index("batch")
    at_r = lax.axis_index("rows")
    counter = [0]
    pending = []

    def remote(src, dst, bat, row):
        i = counter[0]
        counter[0] += 1
        c = pltpu.make_async_remote_copy(
            src_ref=src, dst_ref=dst, send_sem=sems.at[i], recv_sem=rsems.at[i],
            device_id=(bat, row), device_id_type=MESH,
        )
        c.start()
        pending.append(c)
        return c

    def bit_of(s):
        return (at_r // (1 << s)) % 2

    def partner(s):
        return at_r + (1 - 2 * bit_of(s)) * (1 << s)

    barrier = pltpu.get_barrier_semaphore()
    for k in range(1, nrow):
        pl.semaphore_signal(barrier, inc=1, device_id=(at_b, lax.rem(at_r + k, nrow)), device_id_type=MESH)
    for k in range(1, nbat):
        pl.semaphore_signal(barrier, inc=1, device_id=(lax.rem(at_b + k, nbat), at_r), device_id_type=MESH)

    cot_copy = pltpu.make_async_copy(cot_hbm.at[0], cot, lsems.at[0])
    cot_copy.start()

    ktv = kt_ref[...]
    own = []
    for tap in range(9):
        own.append(ktv[:, tap * (CIN + HID) + CIN : (tap + 1) * (CIN + HID)])
    for tap in range(9):
        own.append(ktv[:, tap * (CIN + HID) : tap * (CIN + HID) + CIN])
    own.append(jnp.zeros((UNIT, FPAD - 9 * CIN), F32))
    own = jnp.concatenate(own, axis=1).astype(BF16)

    hi = [bit_of(lo_bits + hi_bits - 1 - s) for s in range(hi_bits)]
    wt[(at_b, *hi)] = own
    sm1[0, at_r] = small_ref[...]
    pl.semaphore_wait(barrier, nrow - 1 + nbat - 1)

    def small_rows(i):
        return [
            remote(sm1.at[i, at_r], sm1.at[i, at_r], at_b, lax.rem(at_r + k, nrow)) for k in range(1, nrow)
        ]

    def small_batch(i, first):
        for c in first:
            c.wait_recv()
        total = sm1[i, 0]
        for k in range(1, nrow):
            total = total + sm1[i, k]
        sm2[i, at_b] = total
        return [
            remote(sm2.at[i, at_b], sm2.at[i, at_b], lax.rem(at_b + k, nbat), at_r) for k in range(1, nbat)
        ]

    def small_done(i, second):
        for c in second:
            c.wait_recv()
        total = sm2[i, 0]
        for k in range(1, nbat):
            total = total + sm2[i, k]
        return total

    lanes = [(HALL, KALL), (0, HALL)]

    def gather_low():
        for s in range(lo_bits):
            dst = lo_recv[lo_bits + s]
            src = lo_send[s]
            src[...] = wt[(at_b, *hi)].astype(BF16)
            c = remote(src, dst, at_b, partner(s))
            c.wait_recv()
            wt[(at_b, *hi)] = wt[(at_b, *hi)] + dst[...]

    def gather_batch(part):
        lo, up = lanes[part]
        ref = wt.at[(at_b, *hi, slice(None), pl.ds(lo, up - lo))]
        return [remote(ref, ref, lax.rem(at_b + k, nbat), at_r) for k in range(1, nbat)]

    def gather_rows(part, s):
        lo, up = lanes[part]
        n_own = hi_bits - s
        idx = (slice(None),) + (slice(None),) * s + tuple(hi[s:]) + (slice(None), pl.ds(lo, up - lo))
        ref = wt.at[idx]
        del n_own
        return remote(ref, ref, at_b, partner(lo_bits + hi_bits - 1 - s))

    gather_low()
    first = small_rows(0)
    g_batch = [gather_batch(p) for p in range(2)]

    crop_h = crop_ref[0, 0]
    crop_w = crop_ref[0, 1]
    row0 = at_r * rows_n
    has_up = (at_r > 0).astype(F32)
    has_down = (at_r < nrow - 1).astype(F32)
    up_r = lax.rem(at_r + nrow - 1, nrow)
    down_r = lax.rem(at_r + 1, nrow)

    rr3 = lax.broadcasted_iota(jnp.int32, (CIN, rows_n, WID), 1) + row0
    cc3 = lax.broadcasted_iota(jnp.int32, (CIN, rows_n, WID), 2)
    live3 = (rr3 < crop_h) & (cc3 < crop_w)
    for t in range(frames_n):
        masked = jnp.where(live3, frames_ref[0, t].astype(F32), 0.0)
        fr[t, 1 : rows_n + 1] = jnp.swapaxes(masked, 0, 1)
        fhalo_s[0, t] = fr[t, 1].astype(BF16)
        fhalo_s[1, t] = fr[t, rows_n].astype(BF16)
    f_up = remote(fhalo_s.at[0], fhalo_r.at[1], at_b, up_r)
    f_down = remote(fhalo_s.at[1], fhalo_r.at[0], at_b, down_r)

    lane = lax.broadcasted_iota(jnp.int32, (CIN, WID), 1)

    def lane_shift(v, by):
        at = lax.broadcasted_iota(jnp.int32, v.shape, 1)
        if by > 0:
            return jnp.where(at == WID - 1, 0.0, pltpu.roll(v, WID - 1, 1))
        return jnp.where(at == 0, 0.0, pltpu.roll(v, 1, 1))

    def row_shift(v, by):
        at = lax.broadcasted_iota(jnp.int32, v.shape, 0)
        if by > 0:
            return jnp.where(at == WID - 1, 0.0, pltpu.roll(v, WID - 1, 0))
        return jnp.where(at == 0, 0.0, pltpu.roll(v, 1, 0))

    def frame_cols(t, rr):
        v = fr[t, rr]
        three = jnp.concatenate([lane_shift(v, -1), v, lane_shift(v, 1)], axis=0)
        xt[t, WIDE : WIDE + FEAT, pl.ds(pl.multiple_of(rr * WID, WID), WID)] = three.astype(BF16)

    def frame_cols_all(rr, carry):
        for t in range(frames_n):
            frame_cols(t, rr)
        return carry

    lax.fori_loop(1, rows_n + 1, frame_cols_all, 0)
    second = small_batch(0, first)
    for c in g_batch[0]:
        c.wait_recv()
    g_rows = [[], []]

    def next_rows(part, s):
        if s > 0:
            g_rows[part][s - 1].wait_recv()
        elif part == 1:
            for c in g_batch[1]:
                c.wait_recv()
        if s < hi_bits:
            g_rows[part].append(gather_rows(part, s))

    next_rows(0, 0)
    f_up.wait_recv()
    f_down.wait_recv()
    for t in range(frames_n):
        fr[t, 0] = fhalo_r[0, t].astype(F32) * has_up
        fr[t, rows_n + 1] = fhalo_r[1, t].astype(F32) * has_down
        frame_cols(t, 0)
        frame_cols(t, rows_n + 1)
    next_rows(1, 0)

    def frame_pixels(t):
        def one(rr, carry):
            parts = [
                xt[t, WIDE : WIDE + FEAT, pl.ds(pl.multiple_of((rr + a) * WID, WID), WID)].astype(F32)
                for a in range(3)
            ]
            parts.append(jnp.zeros((FPAD - 9 * CIN, WID), F32))
            gpre[t, pl.ds(pl.multiple_of(rr * WID, WID), WID), 0:FPAD] = (
                jnp.concatenate(parts, axis=0).T.astype(BF16)
            )
            return carry

        lax.fori_loop(0, rows_n, one, 0)

    frame_pixels(0)
    for s in range(1, hi_bits + 1):
        next_rows(0, s)
        if s <= hi_bits:
            next_rows(1, s)
        if s < frames_n:
            frame_pixels(s)
    for t in range(hi_bits + 1, frames_n):
        frame_pixels(t)

    small = small_done(0, second)
    consts[...] = small
    peep = [consts[i : i + 1, :] for i in range(3)]
    bias = [consts[4 + i : 5 + i, :] for i in range(4)]

    def cat_wt(lo, up):
        v = wt[(slice(None),) * (2 + hi_bits) + (pl.ds(lo, up - lo),)]
        return v.reshape(GATES, up - lo)

    wft[...] = cat_wt(HALL, KALL).astype(F32).T.astype(BF16)

    sub_iota = lax.broadcasted_iota(jnp.int32, (SUB, HID), 0)

    def live_cols(rr):
        return jnp.where(row0 + rr < crop_h, crop_w, 0)

    def place_state(t, v, at):
        three = [row_shift(v, -1), v, row_shift(v, 1)]
        for j in range(3):
            sc[t, at, :, j * HID : (j + 1) * HID] = three[j].astype(BF16)
        vt = v.T
        three = [lane_shift(vt, -1), vt, lane_shift(vt, 1)]
        for j in range(3):
            xt[t + 1, j * HID : (j + 1) * HID, pl.ds(pl.multiple_of(at * WID, WID), WID)] = three[j].astype(BF16)

    def forward_row(t, rr):
        limit = live_cols(rr)
        for j in range(WID // SUB):
            sl = pl.ds(pl.multiple_of(rr * WID + j * SUB, SUB), SUB)
            live = sub_iota + j * SUB < limit
            zi = gates[t, sl, 0:HID] + bias[0]
            zc = gates[t, sl, 2 * HID : 3 * HID] + bias[2]
            zo = gates[t, sl, 3 * HID :] + bias[3]
            if t > 0:
                prev = cells[t - 1, sl, :]
                zf = gates[t, sl, HID : 2 * HID] + bias[1] + peep[1] * prev
                zi = zi + peep[0] * prev
                gf = sigmoid(zf)
                gates[t, sl, HID : 2 * HID] = gf
            gi = sigmoid(zi)
            gc = jnp.tanh(zc)
            c = gi * gc
            if t > 0:
                c = c + gf * prev
            c = jnp.where(live, c, 0.0)
            go = sigmoid(zo + peep[2] * c)
            gates[t, sl, 0:HID] = gi
            gates[t, sl, 2 * HID : 3 * HID] = gc
            gates[t, sl, 3 * HID :] = go
            cells[t, sl, :] = c
            srow[j * SUB : (j + 1) * SUB, :] = jnp.where(live, go * jnp.tanh(c), 0.0)
        if t < frames_n - 1:
            place_state(t, srow[...], rr + 1)
        else:
            hlast[pl.ds(rr, 1)] = srow[...].astype(BF16)[None]

    CH = 4

    def forward_chunk(t, m):
        px = pl.ds(pl.multiple_of(m * CH * WID, CH * WID), CH * WID)
        xf = gpre[t, px, 0:FPAD]
        if t > 0:
            parts = [
                sc[t - 1, pl.ds(m * CH + a, CH)].reshape(CH * WID, WIDE) for a in range(3)
            ]
            x = jnp.concatenate(parts + [xf], axis=1)
            gates[t, px, :] = mm(x, cat_wt(0, KALL), NT)
        else:
            gates[t, px, :] = mm(xf, cat_wt(HALL, KALL), NT)

        def one(i, carry):
            forward_row(t, m * CH + i)
            return carry

        lax.fori_loop(0, CH, one, 0)

    nchunk = rows_n // CH
    hid_copies = []
    halo = None
    for t in range(frames_n):
        lax.fori_loop(1, nchunk - 1, lambda m, c: (forward_chunk(t, m), c)[1], 0)
        if halo is not None:
            halo[0].wait_recv()
            halo[1].wait_recv()
            place_state(t - 1, shalo_r[t - 1, 0].astype(F32) * has_up, 0)
            place_state(t - 1, shalo_r[t - 1, 1].astype(F32) * has_down, rows_n + 1)
        lax.fori_loop(0, 2, lambda m, c: (forward_chunk(t, m * (nchunk - 1)), c)[1], 0)
        if t < frames_n - 1:
            mid = pl.ds(HID, HID)
            halo = (
                remote(sc.at[t, 1, :, mid], shalo_r.at[t, 1], at_b, up_r),
                remote(sc.at[t, rows_n, :, mid], shalo_r.at[t, 0], at_b, down_r),
            )
            c = pltpu.make_async_copy(sc.at[t, pl.ds(1, rows_n), :, mid], hid_hbm.at[0, t], lsems.at[1 + t])
        else:
            c = pltpu.make_async_copy(hlast, hid_hbm.at[0, t], lsems.at[1 + t])
        c.start()
        hid_copies.append(c)

    cot_copy.wait()
    sums[...] = jnp.zeros_like(sums)

    def fold(v):
        return jnp.sum(v.reshape(SUB // 8, 8, HID), axis=0)

    def backward_row(t, rr):
        limit = live_cols(rr)
        parts = [None] * 7
        for j in range(WID // SUB):
            sl = pl.ds(pl.multiple_of(rr * WID + j * SUB, SUB), SUB)
            live = sub_iota + j * SUB < limit
            gi = gates[t, sl, 0:HID]
            gc = gates[t, sl, 2 * HID : 3 * HID]
            go = gates[t, sl, 3 * HID :]
            c = cells[t, sl, :]
            sq = jnp.tanh(c)
            total = cot[t, rr, j * SUB : (j + 1) * SUB, :].astype(F32)
            if t < frames_n - 1:
                total = total + gs[rr + 1, j * SUB : (j + 1) * SUB, :]
            total = jnp.where(live, total, 0.0)
            tgo = total * go
            d_out = tgo * sq * (1.0 - go)
            nxt = tgo * (1.0 - sq * sq) + peep[2] * d_out
            if t < frames_n - 1:
                nxt = nxt + gcell[sl, :]
            kept = jnp.where(live, nxt, 0.0)
            kgi = kept * gi
            d_in = kgi * gc * (1.0 - gi)
            d_cand = kgi * (1.0 - gc * gc)
            vals = [d_in, None, d_cand, d_out, None, None, d_out * c]
            if t > 0:
                gf = gates[t, sl, HID : 2 * HID]
                prev = cells[t - 1, sl, :]
                kgf = kept * gf
                d_for = kgf * prev * (1.0 - gf)
                gcell[sl, :] = kgf + peep[0] * d_in + peep[1] * d_for
                vals[1] = d_for
                vals[4] = d_in * prev
                vals[5] = d_for * prev
            gpre[t, sl, 0:HID] = d_in.astype(BF16)
            gpre[t, sl, HID : 2 * HID] = (vals[1] if t > 0 else jnp.zeros_like(d_in)).astype(BF16)
            gpre[t, sl, 2 * HID : 3 * HID] = d_cand.astype(BF16)
            gpre[t, sl, 3 * HID :] = d_out.astype(BF16)
            for i in range(7):
                if vals[i] is not None:
                    f = fold(vals[i])
                    parts[i] = f if parts[i] is None else parts[i] + f
        for i in range(7):
            if parts[i] is not None:
                sums[i] = sums[i] + parts[i]

    def state_chunk(t, m):
        px = pl.ds(pl.multiple_of(m * CH * WID, CH * WID), CH * WID)
        ybuf[...] = mm(gpre[t, px, :], cat_wt(0, HALL), NN)

        def one(i, carry):
            sl = pl.ds(pl.multiple_of(i * WID, WID), WID)
            for a in range(3):
                z = ybuf[sl, a * WIDE + HID : a * WIDE + 2 * HID]
                z = z + row_shift(ybuf[sl, a * WIDE : a * WIDE + HID], 1)
                z = z + row_shift(ybuf[sl, a * WIDE + 2 * HID : (a + 1) * WIDE], -1)
                at = m * CH + i + a
                gs[at] = gs[at] + z
            return carry

        lax.fori_loop(0, CH, one, 0)

    halo = None
    for t in reversed(range(frames_n)):
        lax.fori_loop(1, rows_n - 1, lambda rr, c: (backward_row(t, rr), c)[1], 0)
        if halo is not None:
            halo[0].wait_recv()
            halo[1].wait_recv()
            gs[1] = gs[1] + ghalo_r[t, 0].astype(F32) * has_up
            gs[rows_n] = gs[rows_n] + ghalo_r[t, 1].astype(F32) * has_down
        lax.fori_loop(0, 2, lambda k, c: (backward_row(t, k * (rows_n - 1)), c)[1], 0)
        if t > 0:
            gs[...] = jnp.zeros_like(gs)
            lax.fori_loop(0, 2, lambda k, c: (state_chunk(t, k * (nchunk - 1)), c)[1], 0)
            ghalo_s[t - 1, 0] = gs[0].astype(BF16)
            ghalo_s[t - 1, 1] = gs[rows_n + 1].astype(BF16)
            halo = (
                remote(ghalo_s.at[t - 1, 0], ghalo_r.at[t - 1, 1], at_b, up_r),
                remote(ghalo_s.at[t - 1, 1], ghalo_r.at[t - 1, 0], at_b, down_r),
            )
            lax.fori_loop(1, nchunk - 1, lambda m, c: (state_chunk(t, m), c)[1], 0)

    for i in range(7):
        at = (4 + i) if i < 4 else i - 4
        sm1[1, at_r, at : at + 1, :] = jnp.sum(sums[i], axis=0, keepdims=True)
    sm1[1, at_r, 3:4, :] = jnp.zeros((1, HID), F32)
    first = small_rows(1)

    widths = [WIDE, WIDE, WIDE, FPAD]
    stage = [0] * 4
    flight = [None] * 4
    full = (slice(None),)

    def reduce_step(q):
        s = stage[q]
        ref = acc[q]
        if s > 0 and s <= hi_bits:
            flight[q].wait_recv()
            mine = (full * s) + (hi[hi_bits - s],)
            recv = stage_recv[q * hi_bits + s - 1]
            keep = ref[s - 1][full * (1 + hi_bits - s) + (hi[hi_bits - s],)]
            ref[s][...] = keep + recv[...].astype(F32)
            del mine
        if s < hi_bits:
            away = 1 - hi[hi_bits - 1 - s]
            snd = stage_send[q * hi_bits + s]
            snd[...] = ref[s][full * (hi_bits - s) + (away,)].astype(BF16)
            flight[q] = remote(snd, stage_recv[q * hi_bits + s], at_b, partner(lo_bits + s))
        elif s == hi_bits:
            snd = last_send[q]
            snd[...] = ref[s][...].astype(BF16)
            flight[q] = [
                remote(snd.at[lax.rem(at_b + k, nbat)], last_recv[q].at[k], lax.rem(at_b + k, nbat), at_r)
                for k in range(1, nbat)
            ]
        elif s == hi_bits + 1:
            for c in flight[q]:
                c.wait_recv()
            total = ref[hi_bits][at_b]
            for k in range(1, nbat):
                total = total + last_recv[q][k].astype(F32)
            if q < 3:
                for j in range(3):
                    tap = 3 * q + j
                    at = tap * (CIN + HID) + CIN
                    nat[:, at : at + HID] = total[:, j * HID : (j + 1) * HID]
            else:
                for tap in range(9):
                    at = tap * (CIN + HID)
                    nat[:, at : at + CIN] = total[:, tap * CIN : (tap + 1) * CIN]
        stage[q] = s + 1

    facc[...] = jnp.zeros_like(facc)
    g0 = [xt[0, WIDE : WIDE + FEAT, a * WID : a * WID + pix] for a in range(3)]
    facc[0 : 9 * CIN, :] = mm(jnp.concatenate(g0, axis=0), gpre[0], NN)

    second = None
    for a in range(3):
        total = None
        for t in range(1, frames_n):
            part = mm(xt[t, :, a * WID : a * WID + pix], gpre[t], NN)
            total = part if total is None else total + part
        facc[a * FEAT : (a + 1) * FEAT, :] = facc[a * FEAT : (a + 1) * FEAT, :] + total[WIDE:, :]
        acc[a][0][...] = total[:WIDE, :].T.reshape(acc[a][0].shape)
        for q in range(a):
            reduce_step(q)
        reduce_step(a)
        if a == 0:
            second = small_batch(1, first)
    acc[3][0][...] = facc[...].T.reshape(acc[3][0].shape)
    for q in range(4):
        reduce_step(q)

    def frame_back(t):
        fgb[t] = jnp.zeros(fgb.shape[1:], F32)

        def chunk(m, carry):
            px = pl.ds(pl.multiple_of(m * CH * WID, CH * WID), CH * WID)
            y = mm(wft[0 : 9 * CIN, :], gpre[t, px, :], NT)
            for i in range(CH):
                for a in range(3):
                    part = y[a * FEAT : (a + 1) * FEAT, i * WID : (i + 1) * WID]
                    z = part[CIN : 2 * CIN]
                    z = z + lane_shift(part[0:CIN], 1)
                    z = z + lane_shift(part[2 * CIN :], -1)
                    at = m * CH + i + a
                    fgb[t, at] = fgb[t, at] + z
            return carry

        lax.fori_loop(0, nchunk, chunk, 0)
        bhalo_s[0, t] = fgb[t, 0].astype(BF16)
        bhalo_s[1, t] = fgb[t, rows_n + 1].astype(BF16)

    for t in range(frames_n):
        frame_back(t)
        for q in range(4):
            if stage[q] < hi_bits + 2 and t < frames_n - 1:
                reduce_step(q)
    f_up = remote(bhalo_s.at[0], bhalo_r.at[1], at_b, up_r)
    f_down = remote(bhalo_s.at[1], bhalo_r.at[0], at_b, down_r)
    while any(s < hi_bits + 2 for s in stage):
        for q in range(4):
            if stage[q] < hi_bits + 2:
                reduce_step(q)
    for s in range(lo_bits):
        lo_send[s][...] = nat[...].astype(BF16)
        c = remote(lo_send[s], lo_recv[s], at_b, partner(s))
        c.wait_recv()
        nat[...] = nat[...] + lo_recv[s][...].astype(F32)

    g = nat[:, 0:KROWS]
    rows_own = GATES // (nbat * nrow)
    squares = g * g
    if lo_bits:
        base = lax.rem(at_r, 1 << lo_bits) * rows_own
        ri = lax.broadcasted_iota(jnp.int32, squares.shape, 0)
        squares = jnp.where((ri >= base) & (ri < base + rows_own), squares, 0.0)
    sm1[2, at_r] = jnp.broadcast_to(jnp.sum(squares), (8, HID))
    third = small_rows(2)
    grad_ref[...] = g
    small = small_done(1, second)
    small_out[...] = small
    f_up.wait_recv()
    f_down.wait_recv()
    fourth = small_batch(2, third)
    for t in range(frames_n):
        fgb[t, 1] = fgb[t, 1] + bhalo_r[0, t].astype(F32) * has_up
        fgb[t, rows_n] = fgb[t, rows_n] + bhalo_r[1, t].astype(F32) * has_down
        fg_ref[0, t] = jnp.where(live3, jnp.swapaxes(fgb[t, 1 : rows_n + 1], 0, 1), 0.0)
    squares = small_done(2, fourth) + jnp.sum(small * small)
    norm_out[...] = jnp.sqrt(squares)

    for c in hid_copies:
        c.wait()
    for c in pending:
        c.wait_send()
    del lane


def adamw_update(weight, gradient, first, second, scale):
    clipped = gradient * scale
    first_new = BETA_ONE * first + (1.0 - BETA_ONE) * clipped
    second_new = BETA_TWO * second + (1.0 - BETA_TWO) * clipped * clipped
    first_hat = first_new / (1.0 - BETA_ONE**STEP)
    second_hat = second_new / (1.0 - BETA_TWO**STEP)
    weight_new = weight - LEARN_RATE * (
        first_hat / (jnp.sqrt(second_hat) + ADAM_EPS) + WEIGHT_DECAY * weight
    )
    return (weight_new, first_new, second_new)


def local(
    nbat,
    nrow,
    frames,
    crop_sizes,
    kernel,
    gate_bias,
    peepholes,
    cotangent,
    kernel_first,
    kernel_second,
    bias_first,
    bias_second,
    peep_first,
    peep_second,
):
    frames_n, rows_n = frames.shape[1], frames.shape[3]
    pix = rows_n * WID
    own = kernel.shape[1]
    share = max(1, UNIT // own)
    lo_bits = int(math.log2(share))
    hi_bits = int(math.log2(nrow)) - lo_bits
    at_b = lax.axis_index("batch")
    at_r = lax.axis_index("rows")
    flat = (at_b * nrow + at_r) * own
    pw = peepholes.shape[1]

    kt = kernel.T
    if lo_bits:
        kt = lax.dynamic_update_slice(
            jnp.zeros((UNIT, KROWS), F32), kt, (lax.rem(at_r, share) * own, 0)
        )
    bias_tile = lax.dynamic_update_slice(jnp.zeros((GATES,), F32), gate_bias, (flat,)).reshape(4, HID)
    peep_mine = jnp.where(at_r == 0, peepholes, 0.0)
    peep_tile = lax.dynamic_update_slice(jnp.zeros((4, HID), F32), peep_mine, (0, at_b * pw))
    small = jnp.concatenate([peep_tile, bias_tile], axis=0)

    blocks = (nbat,) + (2,) * hi_bits
    widths = [WIDE, WIDE, WIDE, FPAD]
    vm = functools.partial(pltpu.VMEM)
    stage_shapes = []
    for wide in widths:
        for s in range(hi_bits):
            stage_shapes.append(vm((nbat,) + (2,) * (hi_bits - s - 1) + (UNIT, wide), BF16))
    last_shapes = [vm((nbat, UNIT, wide), BF16) for wide in widths]
    acc_shapes = []
    for wide in widths:
        acc_shapes.append([vm((nbat,) + (2,) * (hi_bits - s) + (UNIT, wide), F32) for s in range(hi_bits + 1)])
    ncopies = (
        3 * (nrow - 1 + nbat - 1)
        + 2 * (nbat - 1 + hi_bits)
        + 4 * (hi_bits + nbat - 1)
        + 4
        + 4 * (frames_n - 1)
        + 2 * lo_bits
    )
    scratch = [
        vm(blocks + (UNIT, KALL), BF16),
        vm((FPAD, GATES), BF16),
        vm((frames_n, rows_n + 2, CIN, WID), F32),
        vm((frames_n, WIDE + FEAT, (rows_n + 2) * WID), BF16),
        vm((frames_n - 1, rows_n + 2, WID, WIDE), BF16),
        vm((frames_n, pix, GATES), F32),
        vm((frames_n, pix, HID), F32),
        vm((frames_n, pix, GATES), BF16),
        vm((pix, HID), F32),
        vm((rows_n + 2, WID, HID), F32),
        vm((4 * WID, HALL), F32),
        vm((frames_n, rows_n + 2, CIN, WID), F32),
        vm((frames_n, rows_n, WID, HID), BF16),
        vm((rows_n, WID, HID), BF16),
        vm((WID, HID), F32),
        vm((8, HID), F32),
        vm((7, 8, HID), F32),
        acc_shapes,
        vm((FPAD, GATES), F32),
        vm((2, frames_n, CIN, WID), BF16),
        vm((2, frames_n, CIN, WID), BF16),
        vm((frames_n - 1, 2, WID, HID), BF16),
        vm((frames_n - 1, 2, WID, HID), BF16),
        vm((frames_n - 1, 2, WID, HID), BF16),
        vm((2, frames_n, CIN, WID), BF16),
        vm((2, frames_n, CIN, WID), BF16),
        vm((UNIT, KALL), F32),
        vm((3, nrow, 8, HID), F32),
        vm((3, nbat, 8, HID), F32),
    ]
    scratch += stage_shapes + stage_shapes + last_shapes + last_shapes
    scratch += [vm((UNIT, KALL), BF16)] * (3 * lo_bits)
    scratch += [
        pltpu.SemaphoreType.DMA((ncopies,)),
        pltpu.SemaphoreType.DMA((ncopies,)),
        pltpu.SemaphoreType.DMA((1 + frames_n,)),
    ]
    smem = pl.BlockSpec(memory_space=pltpu.SMEM)
    vmem = pl.BlockSpec(memory_space=pltpu.VMEM)
    hbm = pl.BlockSpec(memory_space=pl.ANY)
    dims = (nbat, nrow, frames_n, rows_n, hi_bits, lo_bits)
    hidden_seq, frames_grad, kernel_sum, small_sum, norm = pl.pallas_call(
        functools.partial(layer_kernel, dims),
        out_shape=(
            jax.ShapeDtypeStruct(cotangent.shape, BF16),
            jax.ShapeDtypeStruct(frames.shape, F32),
            jax.ShapeDtypeStruct((UNIT, KROWS), F32),
            jax.ShapeDtypeStruct((8, HID), F32),
            jax.ShapeDtypeStruct((8, HID), F32),
        ),
        in_specs=[smem, vmem, vmem, vmem, hbm],
        out_specs=(hbm, vmem, vmem, vmem, vmem),
        scratch_shapes=scratch,
        compiler_params=pltpu.CompilerParams(
            collective_id=0, has_side_effects=True, vmem_limit_bytes=63 << 20
        ),
        name="layer",
    )(crop_sizes, frames, kt, small, cotangent)

    if lo_bits:
        kernel_sum = lax.dynamic_slice_in_dim(kernel_sum, lax.rem(at_r, share) * own, own, 0)
    grad_norm = norm[0, 0]
    scale = jnp.minimum(1.0, CLIP_AT / (grad_norm + 1e-06))
    kernel_grad = kernel_sum.T
    bias_grad = lax.dynamic_slice(small_sum[4:8].reshape(GATES), (flat,), (own,))
    peep_grad = lax.dynamic_slice(small_sum, (0, at_b * pw), (3, pw))
    kernel_new, kernel_first_new, kernel_second_new = adamw_update(
        kernel, kernel_grad, kernel_first, kernel_second, scale
    )
    bias_new, bias_first_new, bias_second_new = adamw_update(
        gate_bias, bias_grad, bias_first, bias_second, scale
    )
    peep_new, peep_first_new, peep_second_new = adamw_update(
        peepholes, peep_grad, peep_first, peep_second, scale
    )
    return (
        hidden_seq,
        frames_grad,
        grad_norm,
        kernel_new,
        kernel_first_new,
        kernel_second_new,
        bias_new,
        bias_first_new,
        bias_second_new,
        peep_new,
        peep_first_new,
        peep_second_new,
    )


def solution(mesh):
    return jax.shard_map(
        functools.partial(local, mesh.shape["batch"], mesh.shape["rows"]),
        mesh=mesh,
        in_specs=(
            P("batch", None, None, "rows", None),
            P("batch", None),
            P(None, ("batch", "rows")),
            P(("batch", "rows")),
            P(None, "batch"),
            P("batch", None, "rows", None, None),
            P(None, ("batch", "rows")),
            P(None, ("batch", "rows")),
            P(("batch", "rows")),
            P(("batch", "rows")),
            P(None, "batch"),
            P(None, "batch"),
        ),
        out_specs=(
            P("batch", None, "rows", None, None),
            P("batch", None, None, "rows", None),
            P(),
            P(None, ("batch", "rows")),
            P(None, ("batch", "rows")),
            P(None, ("batch", "rows")),
            P(("batch", "rows")),
            P(("batch", "rows")),
            P(("batch", "rows")),
            P(None, "batch"),
            P(None, "batch"),
            P(None, "batch"),
        ),
        check_vma=False,
    )
```

time: 669 us -> 131 us (0.20); the launches traced: 660 us -> 130 us
  matrix products: 273 us -> 0 us
  waiting for transfers between devices: 136 us -> 0 us
  Pallas kernels: 0 us -> 117 us
  blocking collectives: 114 us -> 0 us
  other arithmetic: 48.9 us -> 5 us
  starting transfers between devices: 37.2 us -> 0 us
  local copies, waits for them, and re-layouts: 32.1 us -> 7.01 us
  between operations: 19.4 us -> 1.46 us
    dot_general x108 -> x0, matrix products: 273 us -> none  [the longest x36 124 us: local(): jnp.einsum('nhwc,cg->nhwg', window, tap_weights[tap_index], preferred_ele...]
    pallas_call x0 -> x1, Pallas kernels: none -> 117 us  [local(): pl.pallas_call(functools.partial(layer_kernel, dims), out_shape=(jax.Shap...]
    reduce_scatter x2 -> x0, waiting for transfers between devices: 77.8 us -> none  [the longest x1 56.3 us: local(): lax.psum_scatter(kernel_local, 'batch', scatter_dimension=1, tiled=True)]
    unnamed x7 -> x0, waiting for transfers between devices: 49.5 us -> none
    unnamed x1 -> x0, blocking collectives: 40.7 us -> none
    psum x1 -> x0, blocking collectives: 39.3 us -> none  [local(): lax.psum(owned_squares, ('batch', 'rows'))]
    ppermute x16 -> x0, starting transfers between devices: 36.8 us -> none  [the longest x8 25.7 us: padded(): lax.ppermute(tail, axis, [(i, (i + 1) % count) for i in range(ends)])]
    all_gather x2 -> x0, blocking collectives: 34.1 us -> none  [the longest x1 26.9 us: local(): peep_whole = lax.all_gather(peepholes, 'batch', axis=1, tiled=True)]
  transfers between devices with their start and end apart: 21 -> 0, of which waited for: 8 -> 0; matrix products, arithmetic and copies ran while one was open for 11% -> 0% of each run, Pallas kernels for 0% -> 0%
where the time goes in v1:
time: 131 us; the launch traced here: 130 us
  Pallas kernels  117 us (89%)
  local copies, waits for them, and re-layouts  7.01 us (5%)
  other arithmetic  5 us (4%)
  between operations  1.46 us (1%)
    pallas_call x1, Pallas kernels, local(): pl.pallas_call(functools.partial(layer_kernel, dims), out_shape=(jax.Shap...  117 us
    unnamed x22, local copies, waits for them, and re-layouts  4.06 us
    sub x3, other arithmetic, adamw_update(): weight - LEARN_RATE * (first_hat / (jnp.sqrt(second_hat) + ADAM_EPS) + WE...  3.6 us

profile of v1, /device:TPU:0, one launch (start us, length us, event | category | flops | bytes accessed | tf_op | source)
XLA Modules:
  0.0 130.3 jit_solution(7906736141229267608)
XLA Ops:
  0.6 0.0 copy-start.4
  0.7 0.0 copy-start.7
  0.7 0.0 copy-start.1
  0.7 0.0 copy-start.6
  0.7 0.0 copy-start.5
  0.7 0.0 copy-start.9
  0.7 0.0 copy-start.8
  0.7 0.0 copy-start.3
  0.7 0.0 copy-start.2
  0.7 0.8 broadcast_select_fusion
  1.6 0.8 dynamic_update_slice.7
  2.4 0.3 dynamic_update_slice.6
  2.7 0.6 pad_maximum_fusion.small_ref
  3.3 116.8 %layer.1 = (bf16[1,4,16,128,128]{4,3,2,1,0:T(8,128)(2,1)}, f32[1,4,16,16,128]{4,3,2,1,0:T(8,128)}, f32[16,1296]{1,0:T(8,128)}, f32[8,128]{1,0:T(8,128)}, f32[8,128]{1,0:T(8,128)}) custom-call(s32[1,2]{1,0:T(1,128)} %crop_ref.1, bf16[1,4,16,16,128]{4,3,2,1,0:T(8,128)(2,1)} %frames_ref.1, f32[16,1296]{1,0:T(8,128)} %bitcast.12, ...), custom_call_target="tpu_custom_call" | custom-call | tf_op jit(solution)/shard_map/layer/pallas_call | solution.py:726
  120.1 1.2 slice.6
  121.9 0.7 slice_bitcast_fusion
  122.6 0.0 copy-done.7
  122.6 0.0 copy-done.9
  122.6 0.0 copy-done.8
  122.6 0.6 multiply_subtract_fusion.2
  123.2 0.0 copy-done.4
  123.2 0.0 copy-done.6
  123.3 0.0 copy-done.5
  123.3 1.4 %multiply_subtract_fusion.1 = (f32[3,16]{1,0:T(4,128)}, f32[3,16]{1,0:T(4,128)}, f32[3,16]{1,0:T(4,128)}) fusion(f32[3,16]{1,0:T(4,128)S(1)} %copy-done.4, f32[]{:T(128)S(6)} %min_shard_map.3, f32[8,128]{1,0:T(8,128)} %get-tuple-element.21, s32[]{:T(128)S(6)} %select_n.18, f32[3,16]{1,0:T(4,128)S(1)} %copy-done.5, f32[3,16]{1,0:T(4,128)S(1)} %copy-done.6), kind=kLoop, calls=%fused_computation.8 | loop fusion | flops 768 | bytes 1352 | tf_op jit(solution)/shard_map/sub | solution.py:622
  124.6 0.0 copy-done.1
  124.6 0.0 copy-done.3
  124.6 0.0 copy-done.2
  124.6 1.6 %multiply_subtract_fusion = (f32[1296,16]{0,1:T(8,128)}, f32[1296,16]{0,1:T(8,128)}, f32[1296,16]{0,1:T(8,128)}) fusion(f32[1296,16]{0,1:T(8,128)S(1)} %copy-done.1, f32[16,1296]{1,0:T(8,128)} %get-tuple-element.20, f32[]{:T(128)S(6)} %min_shard_map.3, f32[1296,16]{0,1:T(8,128)S(1)} %copy-done.2, f32[1296,16]{0,1:T(8,128)S(1)} %copy-done.3), kind=kLoop, calls=%fused_computation.4 | loop fusion | flops 331776 | bytes 580612 | tf_op jit(solution)/shard_map/sub | solution.py:622
  126.2 0.0 copy-start
  126.3 3.2 %copy.28 = bf16[1,4,16,128,128]{4,3,2,1,0:T(8,128)(2,1)} copy(bf16[1,4,16,128,128]{4,3,2,1,0:T(8,128)(2,1)} %get-tuple-element.43) | data formatting | bytes 4194304
  129.5 0.0 copy-done
  129.5 0.8 copy.29
  (2 shorter events, 0.0 us)
Async XLA Ops:
  0.6 122.6 %copy-start.4 = (f32[3,16]{1,0:T(4,128)S(1)}, f32[3,16]{1,0:T(4,128)}, u32[]{:S(2)}) copy-start(f32[3,16]{1,0:T(4,128)} %param.16) | copy-start | bytes 580
  0.7 122.0 %copy-start.7 = (f32[16]{0:T(128)S(1)}, f32[16]{0:T(128)}, u32[]{:S(2)}) copy-start(f32[16]{0:T(128)} %param.15) | copy-start | bytes 196
  0.7 123.9 %copy-start.1 = (f32[1296,16]{0,1:T(8,128)S(1)}, f32[1296,16]{0,1:T(8,128)}, u32[]{:S(2)}) copy-start(f32[1296,16]{0,1:T(8,128)} %param.14) | copy-start | bytes 248836
  0.7 122.6 %copy-start.6 = (f32[3,16]{1,0:T(4,128)S(1)}, f32[3,16]{1,0:T(4,128)}, u32[]{:S(2)}) copy-start(f32[3,16]{1,0:T(4,128)} %param.23) | copy-start | bytes 580
  0.7 122.6 %copy-start.5 = (f32[3,16]{1,0:T(4,128)S(1)}, f32[3,16]{1,0:T(4,128)}, u32[]{:S(2)}) copy-start(f32[3,16]{1,0:T(4,128)} %param.22) | copy-start | bytes 580
  0.7 121.9 %copy-start.9 = (f32[16]{0:T(128)S(1)}, f32[16]{0:T(128)}, u32[]{:S(2)}) copy-start(f32[16]{0:T(128)} %param.21) | copy-start | bytes 196
  0.7 121.9 %copy-start.8 = (f32[16]{0:T(128)S(1)}, f32[16]{0:T(128)}, u32[]{:S(2)}) copy-start(f32[16]{0:T(128)} %param.20) | copy-start | bytes 196
  0.7 123.9 %copy-start.3 = (f32[1296,16]{0,1:T(8,128)S(1)}, f32[1296,16]{0,1:T(8,128)}, u32[]{:S(2)}) copy-start(f32[1296,16]{0,1:T(8,128)} %param.19) | copy-start | bytes 248836
  0.7 123.9 %copy-start.2 = (f32[1296,16]{0,1:T(8,128)S(1)}, f32[1296,16]{0,1:T(8,128)}, u32[]{:S(2)}) copy-start(f32[1296,16]{0,1:T(8,128)} %param.18) | copy-start | bytes 248836
  126.2 3.2 %copy-start = (f32[1,4,16,16,128]{4,3,2,1,0:T(8,128)S(1)}, f32[1,4,16,16,128]{4,3,2,1,0:T(8,128)}, u32[]{:S(2)}) copy-start(f32[1,4,16,16,128]{4,3,2,1,0:T(8,128)} %get-tuple-element.44) | copy-start | bytes 1572868

commit v2 on v1

v2 whole, which is shorter than its diff:
```python
import functools

import jax
import jax.numpy as jnp
from jax import lax
from jax.experimental import pallas as pl
from jax.experimental.pallas import tpu as pltpu
from jax.sharding import PartitionSpec as P

CIN = 16
HID = 128
GATES = 512
KROWS = 1296
WID = 128
STEP = 5
CLIP_AT = 0.02
LEARN_RATE = 0.02
BETA_ONE = 0.9
BETA_TWO = 0.999
WEIGHT_DECAY = 0.01
ADAM_EPS = 1e-08

F32 = jnp.float32
BF16 = jnp.bfloat16
MESH = pl.DeviceIdType.MESH
NT = (((1,), (1,)), ((), ()))
NN = (((1,), (0,)), ((), ()))

WIDE = 3 * HID
HALL = 3 * WIDE
FEAT = 3 * CIN
FPAD = 256
KALL = HALL + FPAD
PART = 512
SUB = 32
UNIT = 16


def sigmoid(v):
    return 0.5 * jnp.tanh(0.5 * v) + 0.5


def mm(a, b, dims):
    return lax.dot_general(a, b, dims, preferred_element_type=F32)


def layer_kernel(
    dims,
    crop_ref,
    frames_ref,
    kt_ref,
    bias_ref,
    peep_ref,
    cot_hbm,
    hid_hbm,
    fg_hbm,
    grad_ref,
    small_out,
    norm_out,
    wt,
    wft,
    fr,
    xt,
    sc,
    gates,
    cells,
    gpre,
    gs,
    cot,
    srow,
    consts,
    sums,
    acc,
    fzero,
    fgo,
    fhalo_s,
    fhalo_r,
    shalo_r,
    ghalo_s,
    ghalo_r,
    bhalo_s,
    bhalo_r,
    nat,
    *rest,
):
    nbat, nrow, frames_n, rows_n, nfar, nmid, ncore, nlow = dims
    pix = rows_n * WID
    rest = list(rest)
    core_send, core_recv, mid_send, mid_recv, far_send, far_recv = (
        [rest.pop(0) for _ in range(3)] for _ in range(6)
    )
    small_bufs = [rest.pop(0) for _ in range(4)]
    low_send, low_recv = rest.pop(0), rest.pop(0)
    sems = rest.pop(0)
    rsems = rest.pop(0)
    lsems = rest.pop(0)

    at_b = lax.axis_index("batch")
    at_r = lax.axis_index("rows")
    counter = [0]
    pending = []

    def remote(src, dst, bat, row):
        i = counter[0]
        counter[0] += 1
        c = pltpu.make_async_remote_copy(
            src_ref=src, dst_ref=dst, send_sem=sems.at[i], recv_sem=rsems.at[i],
            device_id=(bat, row), device_id_type=MESH,
        )
        c.start()
        pending.append(c)
        return c

    far, near = at_b // 2, at_b % 2
    low = at_r % nlow
    core = (at_r // nlow) % ncore
    half = nmid // 2
    mid = near * half + at_r // (nlow * ncore)

    def device(f, m, c, w):
        return (f * 2 + m // half, ((m % half) * ncore + c) * nlow + w)

    def far_peer(k):
        return device(lax.rem(far + k, nfar), mid, core, low)

    def mid_peer(k):
        return device(far, lax.rem(mid + k, nmid), core, low)

    def core_peer(k):
        return device(far, mid, lax.rem(core + k, ncore), low)

    def low_peer(k):
        return device(far, mid, core, lax.rem(low + k, nlow))

    groups = [(nfar, far_peer, far), (nmid, mid_peer, mid), (ncore, core_peer, core), (nlow, low_peer, low)]
    up_r = lax.rem(at_r + nrow - 1, nrow)
    down_r = lax.rem(at_r + 1, nrow)

    barrier = pltpu.get_barrier_semaphore()
    greeted = 2
    pl.semaphore_signal(barrier, inc=1, device_id=(at_b, up_r), device_id_type=MESH)
    pl.semaphore_signal(barrier, inc=1, device_id=(at_b, down_r), device_id_type=MESH)
    for size, peer, _ in groups:
        for k in range(1, size):
            pl.semaphore_signal(barrier, inc=1, device_id=peer(k), device_id_type=MESH)
            greeted += 1

    cot_copy = pltpu.make_async_copy(cot_hbm.at[0], cot, lsems.at[0])
    cot_copy.start()

    ktv = kt_ref[...]
    own = []
    for tap in range(9):
        own.append(ktv[:, tap * (CIN + HID) + CIN : (tap + 1) * (CIN + HID)])
    for tap in range(9):
        own.append(ktv[:, tap * (CIN + HID) : tap * (CIN + HID) + CIN])
    own.append(jnp.zeros((UNIT, FPAD - 9 * CIN), F32))
    wt[far, mid, core] = jnp.concatenate(own, axis=1).astype(BF16)

    rows_own = GATES // (nbat * nrow)
    flat = (at_b * nrow + at_r) * rows_own
    peep_own = HID // nbat
    tile_row = lax.broadcasted_iota(jnp.int32, (8, HID), 0)
    consts[...] = jnp.zeros_like(consts)
    consts[0:3, 0:peep_own] = peep_ref[...]
    consts[4:5, 0:rows_own] = bias_ref[...]
    peep_tile = pltpu.roll(jnp.where(tile_row < 3, consts[...], 0.0), at_b * peep_own, 1)
    bias_tile = pltpu.roll(jnp.broadcast_to(consts[4:5, :], (8, HID)), flat % HID, 1)
    bias_tile = jnp.where(tile_row == 4 + flat // HID, bias_tile, 0.0)
    start_tile = jnp.where(at_r == 0, peep_tile, 0.0) + bias_tile

    small_step = [0] * 3
    small_sum = [None] * 3
    small_moving = [None] * 3

    def small_next(i, tile=None):
        s = small_step[i]
        small_step[i] = s + 1
        while s < 4 and groups[s][0] == 1:
            s += 1
            small_step[i] = s + 1
        if tile is None:
            done = s - 1
            while groups[done][0] == 1:
                done -= 1
            for c in small_moving[i]:
                c.wait_recv()
            tile = small_bufs[done][i, 0]
            for k in range(1, groups[done][0]):
                tile = tile + small_bufs[done][i, k]
        if s < 4:
            size, peer, place = groups[s]
            ref = small_bufs[s].at[i, place]
            ref[...] = tile
            small_moving[i] = [remote(ref, ref, *peer(k)) for k in range(1, size)]
            return None
        return tile

    def small_finish(i):
        while True:
            tile = small_next(i)
            if tile is not None:
                return tile

    lanes = [(HALL, KALL), (0, WIDE), (WIDE, 2 * WIDE), (2 * WIDE, HALL)]
    steps = [0] * 4
    moving = [None] * 4

    def gather_low():
        if nlow > 1:
            low_send[...] = wt[far, mid, core]
            copies = [remote(low_send, low_recv.at[0, k - 1], *low_peer(k)) for k in range(1, nlow)]
            total = low_send[...]
            for k in range(1, nlow):
                copies[k - 1].wait_recv()
                total = total + low_recv[0, k - 1]
            wt[far, mid, core] = total

    def gather_step(i):
        lo, up = lanes[i]
        cols = pl.ds(lo, up - lo)
        s = steps[i]
        steps[i] = s + 1
        if 0 < s < 4:
            for c in moving[i]:
                c.wait_recv()
        if s < 3:
            size, peer, _ = groups[s]
            if s == 0:
                ref = wt.at[far, mid, core, :, cols]
            elif s == 1:
                ref = wt.at[:, mid, core, :, cols]
            else:
                ref = wt.at[:, :, core, :, cols]
            moving[i] = [remote(ref, ref, *peer(k)) for k in range(1, size)]

    crop_h = crop_ref[0, 0]
    crop_w = crop_ref[0, 1]
    row0 = at_r * rows_n
    has_up = (at_r > 0).astype(F32)
    has_down = (at_r < nrow - 1).astype(F32)

    rr3 = lax.broadcasted_iota(jnp.int32, (CIN, rows_n, WID), 1) + row0
    cc3 = lax.broadcasted_iota(jnp.int32, (CIN, rows_n, WID), 2)
    live3 = (rr3 < crop_h) & (cc3 < crop_w)
    for t in range(frames_n):
        masked = jnp.where(live3, frames_ref[0, t].astype(F32), 0.0)
        fr[t, 1 : rows_n + 1] = jnp.swapaxes(masked, 0, 1)
        fhalo_s[0, t] = fr[t, 1].astype(BF16)
        fhalo_s[1, t] = fr[t, rows_n].astype(BF16)

    def lane_shift(v, by):
        at = lax.broadcasted_iota(jnp.int32, v.shape, 1)
        if by > 0:
            return jnp.where(at == WID - 1, 0.0, pltpu.roll(v, WID - 1, 1))
        return jnp.where(at == 0, 0.0, pltpu.roll(v, 1, 1))

    def row_shift(v, by):
        at = lax.broadcasted_iota(jnp.int32, v.shape, 0)
        if by > 0:
            return jnp.where(at == WID - 1, 0.0, pltpu.roll(v, WID - 1, 0))
        return jnp.where(at == 0, 0.0, pltpu.roll(v, 1, 0))

    def frame_cols(t, rr):
        v = fr[t, rr]
        three = jnp.concatenate([lane_shift(v, -1), v, lane_shift(v, 1)], axis=0)
        xt[t, WIDE : WIDE + FEAT, pl.ds(pl.multiple_of(rr * WID, WID), WID)] = three.astype(BF16)

    def frame_cols_all(rr, carry):
        for t in range(frames_n):
            frame_cols(t, rr)
        return carry

    def frame_pixels(t, lo, up):
        def one(rr, carry):
            parts = [
                xt[t, WIDE : WIDE + FEAT, pl.ds(pl.multiple_of((rr + a) * WID, WID), WID)].astype(F32)
                for a in range(3)
            ]
            parts.append(jnp.zeros((FPAD - 9 * CIN, WID), F32))
            gpre[t, pl.ds(pl.multiple_of(rr * WID, WID), WID), 0:FPAD] = (
                jnp.concatenate(parts, axis=0).T.astype(BF16)
            )
            return carry

        lax.fori_loop(lo, up, one, 0)

    lax.fori_loop(1, rows_n + 1, frame_cols_all, 0)
    frame_pixels(0, 1, rows_n - 1)

    pl.semaphore_wait(barrier, greeted)
    gather_low()
    gather_step(0)
    small_next(0, start_tile)
    f_up = remote(fhalo_s.at[0], fhalo_r.at[1], at_b, up_r)
    f_down = remote(fhalo_s.at[1], fhalo_r.at[0], at_b, down_r)
    gather_step(1)
    gather_step(2)
    gather_step(3)
    if frames_n > 1:
        frame_pixels(1, 1, rows_n - 1)
    gather_step(0)
    small_next(0)
    f_up.wait_recv()
    f_down.wait_recv()
    for t in range(frames_n):
        fr[t, 0] = fhalo_r[0, t].astype(F32) * has_up
        fr[t, rows_n + 1] = fhalo_r[1, t].astype(F32) * has_down
        frame_cols(t, 0)
        frame_cols(t, rows_n + 1)
    for t in range(min(2, frames_n)):
        frame_pixels(t, 0, 1)
        frame_pixels(t, rows_n - 1, rows_n)
    gather_step(1)
    if frames_n > 2:
        frame_pixels(2, 0, rows_n)
    gather_step(2)
    gather_step(0)
    small_next(0)
    gather_step(3)
    for t in range(3, frames_n):
        frame_pixels(t, 0, rows_n)
    gather_step(0)

    consts[...] = small_finish(0)
    peep = [consts[i : i + 1, :] for i in range(3)]
    bias = [consts[4 + i : 5 + i, :] for i in range(4)]

    def cat_wt(lo, up):
        return wt[:, :, :, :, lo:up].reshape(GATES, up - lo)

    sub_iota = lax.broadcasted_iota(jnp.int32, (SUB, HID), 0)

    def live_cols(rr):
        return jnp.where(row0 + rr < crop_h, crop_w, 0)

    def place_state(t, v, at):
        three = [row_shift(v, -1), v, row_shift(v, 1)]
        for j in range(3):
            sc[t, at, :, j * HID : (j + 1) * HID] = three[j].astype(BF16)
        vt = v.T
        three = [lane_shift(vt, -1), vt, lane_shift(vt, 1)]
        for j in range(3):
            xt[t + 1, j * HID : (j + 1) * HID, pl.ds(pl.multiple_of(at * WID, WID), WID)] = three[j].astype(BF16)

    def forward_row(t, rr):
        limit = live_cols(rr)
        for j in range(WID // SUB):
            sl = pl.ds(pl.multiple_of(rr * WID + j * SUB, SUB), SUB)
            live = sub_iota + j * SUB < limit
            zi = gates[t, sl, 0:HID] + bias[0]
            zc = gates[t, sl, 2 * HID : 3 * HID] + bias[2]
            zo = gates[t, sl, 3 * HID :] + bias[3]
            if t > 0:
                prev = cells[t - 1, sl, :]
                zf = gates[t, sl, HID : 2 * HID] + bias[1] + peep[1] * prev
                zi = zi + peep[0] * prev
                gf = sigmoid(zf)
                gates[t, sl, HID : 2 * HID] = gf
            gi = sigmoid(zi)
            gc = jnp.tanh(zc)
            c = gi * gc
            if t > 0:
                c = c + gf * prev
            c = jnp.where(live, c, 0.0)
            go = sigmoid(zo + peep[2] * c)
            gates[t, sl, 0:HID] = gi
            gates[t, sl, 2 * HID : 3 * HID] = gc
            gates[t, sl, 3 * HID :] = go
            cells[t, sl, :] = c
            srow[j * SUB : (j + 1) * SUB, :] = jnp.where(live, go * jnp.tanh(c), 0.0)
        if t < frames_n - 1:
            place_state(t, srow[...], rr + 1)
        else:
            sc[0, rr + 1, :, 0:HID] = srow[...].astype(BF16)

    CH = 4

    def forward_chunk(t, m):
        px = pl.ds(pl.multiple_of(m * CH * WID, CH * WID), CH * WID)
        xf = gpre[t, px, 0:FPAD]
        if t > 0:
            parts = [
                sc[t - 1, pl.ds(m * CH + a, CH)].reshape(CH * WID, WIDE) for a in range(3)
            ]
            x = jnp.concatenate(parts + [xf], axis=1)
            gates[t, px, :] = mm(x, cat_wt(0, KALL), NT)
        else:
            gates[t, px, :] = mm(xf, cat_wt(HALL, KALL), NT)

        def one(i, carry):
            forward_row(t, m * CH + i)
            return carry

        lax.fori_loop(0, CH, one, 0)

    nchunk = rows_n // CH
    hid_copies = []
    halo = None
    for t in range(frames_n):
        if t == 0:
            for m in range(nchunk):
                forward_chunk(0, m)
                if m < 3:
                    gather_step(1 + m)
            for i in range(1, 4):
                while steps[i] < 4:
                    gather_step(i)
        else:
            lax.fori_loop(1, nchunk - 1, lambda m, c: (forward_chunk(t, m), c)[1], 0)
        if halo is not None:
            halo[0].wait_recv()
            halo[1].wait_recv()
            place_state(t - 1, shalo_r[t - 1, 0].astype(F32) * has_up, 0)
            place_state(t - 1, shalo_r[t - 1, 1].astype(F32) * has_down, rows_n + 1)
        if t > 0:
            lax.fori_loop(0, 2, lambda m, c: (forward_chunk(t, m * (nchunk - 1)), c)[1], 0)
        if t < frames_n - 1:
            center = pl.ds(HID, HID)
            halo = (
                remote(sc.at[t, 1, :, center], shalo_r.at[t, 1], at_b, up_r),
                remote(sc.at[t, rows_n, :, center], shalo_r.at[t, 0], at_b, down_r),
            )
            c = pltpu.make_async_copy(sc.at[t, pl.ds(1, rows_n), :, center], hid_hbm.at[0, t], lsems.at[1 + t])
        else:
            c = pltpu.make_async_copy(
                sc.at[0, pl.ds(1, rows_n), :, pl.ds(0, HID)], hid_hbm.at[0, t], lsems.at[1 + t]
            )
        c.start()
        hid_copies.append(c)

    cot_copy.wait()
    sums[...] = jnp.zeros_like(sums)

    def fold(v):
        return jnp.sum(v.reshape(SUB // 8, 8, HID), axis=0)

    def backward_row(t, rr):
        limit = live_cols(rr)
        parts = [None] * 7
        for j in range(WID // SUB):
            sl = pl.ds(pl.multiple_of(rr * WID + j * SUB, SUB), SUB)
            live = sub_iota + j * SUB < limit
            gi = gates[t, sl, 0:HID]
            gc = gates[t, sl, 2 * HID : 3 * HID]
            go = gates[t, sl, 3 * HID :]
            c = cells[t, sl, :]
            sq = jnp.tanh(c)
            total = cot[t, rr, j * SUB : (j + 1) * SUB, :].astype(F32)
            if t < frames_n - 1:
                total = total + gs[rr + 1, j * SUB : (j + 1) * SUB, :]
            total = jnp.where(live, total, 0.0)
            tgo = total * go
            d_out = tgo * sq * (1.0 - go)
            nxt = tgo * (1.0 - sq * sq) + peep[2] * d_out
            if t < frames_n - 1:
                nxt = nxt + cells[t + 1, sl, :]
            kept = jnp.where(live, nxt, 0.0)
            kgi = kept * gi
            d_in = kgi * gc * (1.0 - gi)
            d_cand = kgi * (1.0 - gc * gc)
            vals = [d_in, None, d_cand, d_out, None, None, d_out * c]
            if t > 0:
                gf = gates[t, sl, HID : 2 * HID]
                prev = cells[t - 1, sl, :]
                kgf = kept * gf
                d_for = kgf * prev * (1.0 - gf)
                cells[t, sl, :] = kgf + peep[0] * d_in + peep[1] * d_for
                vals[1] = d_for
                vals[4] = d_in * prev
                vals[5] = d_for * prev
            gpre[t, sl, 0:HID] = d_in.astype(BF16)
            gpre[t, sl, HID : 2 * HID] = (vals[1] if t > 0 else jnp.zeros_like(d_in)).astype(BF16)
            gpre[t, sl, 2 * HID : 3 * HID] = d_cand.astype(BF16)
            gpre[t, sl, 3 * HID :] = d_out.astype(BF16)
            for i in range(7):
                if vals[i] is not None:
                    f = fold(vals[i])
                    parts[i] = f if parts[i] is None else parts[i] + f
        for i in range(7):
            if parts[i] is not None:
                sums[i] = sums[i] + parts[i]

    def state_chunk(t, m):
        px = pl.ds(pl.multiple_of(m * CH * WID, CH * WID), CH * WID)
        y = mm(gpre[t, px, :], cat_wt(0, HALL), NN)
        for a in range(3):
            buf = acc[a][0]
            buf[..., 0:WIDE] = y[:, a * WIDE : (a + 1) * WIDE].reshape(buf.shape[:-1] + (WIDE,))

        def one(i, carry):
            for a in range(3):
                buf = acc[a][0]
                per = nfar // CH
                three = [
                    buf[pl.ds(i * per, per), :, :, :, j * HID : (j + 1) * HID].reshape(WID, HID)
                    for j in range(3)
                ]
                z = three[1] + row_shift(three[0], 1) + row_shift(three[2], -1)
                at = m * CH + i + a
                gs[at] = gs[at] + z
            return carry

        lax.fori_loop(0, CH, one, 0)

    halo = None
    for t in reversed(range(frames_n)):
        lax.fori_loop(1, rows_n - 1, lambda rr, c: (backward_row(t, rr), c)[1], 0)
        if halo is not None:
            halo[0].wait_recv()
            halo[1].wait_recv()
            gs[1] = gs[1] + ghalo_r[t, 0].astype(F32) * has_up
            gs[rows_n] = gs[rows_n] + ghalo_r[t, 1].astype(F32) * has_down
        lax.fori_loop(0, 2, lambda k, c: (backward_row(t, k * (rows_n - 1)), c)[1], 0)
        if t > 0:
            gs[...] = jnp.zeros_like(gs)
            lax.fori_loop(0, 2, lambda k, c: (state_chunk(t, k * (nchunk - 1)), c)[1], 0)
            ghalo_s[t - 1, 0] = gs[0].astype(BF16)
            ghalo_s[t - 1, 1] = gs[rows_n + 1].astype(BF16)
            halo = (
                remote(ghalo_s.at[t - 1, 0], ghalo_r.at[t - 1, 1], at_b, up_r),
                remote(ghalo_s.at[t - 1, 1], ghalo_r.at[t - 1, 0], at_b, down_r),
            )
            lax.fori_loop(1, nchunk - 1, lambda m, c: (state_chunk(t, m), c)[1], 0)

    rows = [jnp.sum(sums[i], axis=0, keepdims=True) for i in range(7)]
    small_next(1, jnp.concatenate(rows[4:] + [jnp.zeros((1, HID), F32)] + rows[:4], axis=0))

    stage = [0] * 3
    flight = [None] * 3
    parts = [[acc[q][0], acc[q][1] if ncore > 1 else acc[q][0].at[:, :, 0]] for q in range(3)]

    def reduce_step(q):
        s = stage[q]
        stage[q] = s + 1
        first, second = parts[q]
        if s == 0 and ncore > 1:
            core_send[q][...] = first[:, :, 1 - core].astype(BF16)
            flight[q] = [remote(core_send[q], core_recv[q], *core_peer(1))]
        elif s == 1:
            if ncore > 1:
                flight[q][0].wait_recv()
                second[...] = first[:, :, core] + core_recv[q][...].astype(F32)
            flight[q] = []
            for k in range(1, nmid):
                to = lax.rem(mid + k, nmid)
                mid_send[q][k - 1] = second[:, to].astype(BF16)
                flight[q].append(remote(mid_send[q].at[k - 1], mid_recv[q].at[k - 1], *mid_peer(k)))
        elif s == 2:
            total = second[:, mid]
            for k in range(1, nmid):
                flight[q][k - 1].wait_recv()
                total = total + mid_recv[q][k - 1].astype(F32)
            second[:, mid] = total
            far_send[q][...] = total.astype(BF16)
            flight[q] = []
            for k in range(1, nfar):
                to = lax.rem(far + k, nfar)
                flight[q].append(remote(far_send[q].at[to], far_recv[q].at[k - 1], *far_peer(k)))
        elif s == 3:
            total = second[far, mid]
            for k in range(1, nfar):
                flight[q][k - 1].wait_recv()
                total = total + far_recv[q][k - 1].astype(F32)
            for j in range(3):
                at = (3 * q + j) * (CIN + HID)
                nat[:, at : at + CIN] = total[:, WIDE + j * CIN : WIDE + (j + 1) * CIN]
                nat[:, at + CIN : at + CIN + HID] = total[:, j * HID : (j + 1) * HID]

    g0 = [xt[0, WIDE : WIDE + FEAT, a * WID : a * WID + pix] for a in range(3)]
    fzero[...] = mm(jnp.concatenate(g0, axis=0), gpre[0], NN)

    for a in range(3):
        total = None
        for t in range(1, frames_n):
            part = mm(xt[t, :, a * WID : a * WID + pix], gpre[t], NN)
            total = part if total is None else total + part
            if t == 1 and a > 0:
                if a > 1:
                    reduce_step(a - 2)
                reduce_step(a - 1)
                small_next(1)
        extra = total[WIDE:, :] + fzero[a * FEAT : (a + 1) * FEAT, :]
        whole = jnp.concatenate([total[:WIDE, :], extra, jnp.zeros((PART - WIDE - FEAT, GATES), F32)], axis=0)
        acc[a][0][...] = whole.T.reshape(acc[a][0].shape)
        reduce_step(a)

    fgb = fr

    def frame_back(t):
        fgb[t] = jnp.zeros(fgb.shape[1:], F32)

        def chunk(m, carry):
            px = pl.ds(pl.multiple_of(m * CH * WID, CH * WID), CH * WID)
            y = mm(wft[0 : 9 * CIN, :], gpre[t, px, :], NT)
            for i in range(CH):
                for a in range(3):
                    part = y[a * FEAT : (a + 1) * FEAT, i * WID : (i + 1) * WID]
                    z = part[CIN : 2 * CIN]
                    z = z + lane_shift(part[0:CIN], 1)
                    z = z + lane_shift(part[2 * CIN :], -1)
                    at = m * CH + i + a
                    fgb[t, at] = fgb[t, at] + z
            return carry

        lax.fori_loop(0, nchunk, chunk, 0)
        bhalo_s[0, t] = fgb[t, 0].astype(BF16)
        bhalo_s[1, t] = fgb[t, rows_n + 1].astype(BF16)

    wft[...] = cat_wt(HALL, KALL).astype(F32).T.astype(BF16)
    after = [[2], [1, 0], [], []]
    for t in range(frames_n):
        frame_back(t)
        for q in after[t] if t < 4 else []:
            reduce_step(q)
    f_up = remote(bhalo_s.at[0], bhalo_r.at[1], at_b, up_r)
    f_down = remote(bhalo_s.at[1], bhalo_r.at[0], at_b, down_r)
    for q in (2, 1, 0):
        while stage[q] < 3:
            reduce_step(q)
    for q in range(3):
        while stage[q] < 4:
            reduce_step(q)
    if nlow > 1:
        low_send[...] = nat[...].astype(BF16)
        copies = [remote(low_send, low_recv.at[1, k - 1], *low_peer(k)) for k in range(1, nlow)]
        total = nat[...]
        for k in range(1, nlow):
            copies[k - 1].wait_recv()
            total = total + low_recv[1, k - 1].astype(F32)
        nat[...] = total

    g = nat[:, 0:KROWS]
    squares = g * g
    if nlow > 1:
        base = low * rows_own
        ri = lax.broadcasted_iota(jnp.int32, squares.shape, 0)
        squares = jnp.where((ri >= base) & (ri < base + rows_own), squares, 0.0)
    small_next(2, jnp.broadcast_to(jnp.sum(squares), (8, HID)))
    grad_ref[...] = g
    small = small_finish(1)
    small_out[...] = small
    f_up.wait_recv()
    f_down.wait_recv()
    small_next(2)
    for t in range(frames_n):
        fgb[t, 1] = fgb[t, 1] + bhalo_r[0, t].astype(F32) * has_up
        fgb[t, rows_n] = fgb[t, rows_n] + bhalo_r[1, t].astype(F32) * has_down
        fgo[t] = jnp.where(live3, jnp.swapaxes(fgb[t, 1 : rows_n + 1], 0, 1), 0.0)
    c = pltpu.make_async_copy(fgo, fg_hbm.at[0], lsems.at[1 + frames_n])
    c.start()
    hid_copies.append(c)
    squares = small_finish(2) + jnp.sum(small * small)
    norm_out[...] = jnp.sqrt(squares)

    for c in hid_copies:
        c.wait()
    for c in pending:
        c.wait_send()


def adamw_update(weight, gradient, first, second, scale):
    clipped = gradient * scale
    first_new = BETA_ONE * first + (1.0 - BETA_ONE) * clipped
    second_new = BETA_TWO * second + (1.0 - BETA_TWO) * clipped * clipped
    first_hat = first_new / (1.0 - BETA_ONE**STEP)
    second_hat = second_new / (1.0 - BETA_TWO**STEP)
    weight_new = weight - LEARN_RATE * (
        first_hat / (jnp.sqrt(second_hat) + ADAM_EPS) + WEIGHT_DECAY * weight
    )
    return (weight_new, first_new, second_new)


def update_kernel(
    dims, hid_in, fg_in, norm_ref, sum_ref, small_ref,
    k_ref, b_ref, p_ref, k1_ref, k2_ref, b1_ref, b2_ref, p1_ref, p2_ref,
    hid_out, fg_out, norm_out, ko, k1o, k2o, bo, b1o, b2o, po, p1o, p2o, hid_buf, fg_buf, sems,
):
    nbat, nrow = dims
    frames_n = hid_buf.shape[0]
    fetch, put = [], []
    for t in range(frames_n):
        for i, (src, buf, dst) in enumerate(((hid_in, hid_buf, hid_out), (fg_in, fg_buf, fg_out))):
            fetch.append(pltpu.make_async_copy(src.at[0, t], buf.at[t], sems.at[i, t]))
            put.append(pltpu.make_async_copy(buf.at[t], dst.at[0, t], sems.at[2 + i, t]))
    for c in fetch:
        c.start()
    at_b = lax.axis_index("batch")
    at_r = lax.axis_index("rows")
    norm_out[0, 0] = norm_ref[0, 0]
    norm = jnp.full((1, HID), norm_ref[0, 0], F32)
    scale = jnp.minimum(1.0, CLIP_AT / (norm + 1e-06))
    small = small_ref[...]
    rows_own = b_ref.shape[1]
    peep_own = p_ref.shape[1]
    flat = (at_b * nrow + at_r) * rows_own
    lane_back = lax.rem(HID - flat % HID, HID)
    tile_row = lax.broadcasted_iota(jnp.int32, (8, HID), 0)
    picked = jnp.where(tile_row == 4 + flat // HID, small, 0.0)
    picked = jnp.sum(pltpu.roll(picked, lane_back, 1), axis=0, keepdims=True)
    new = adamw_update(b_ref[...], picked[:, 0:rows_own], b1_ref[...], b2_ref[...], scale[:, 0:rows_own])
    bo[...], b1o[...], b2o[...] = new
    shifted = pltpu.roll(small, lax.rem(HID - at_b * peep_own, HID), 1)
    new = adamw_update(p_ref[...], shifted[0:3, 0:peep_own], p1_ref[...], p2_ref[...], scale[:, 0:peep_own])
    po[...], p1o[...], p2o[...] = new
    new = adamw_update(k_ref[...], sum_ref[...], k1_ref[...], k2_ref[...], scale[:, 0:1])
    ko[...], k1o[...], k2o[...] = new
    for i in range(len(fetch)):
        fetch[i].wait()
        put[i].start()
    for c in put:
        c.wait()


def local(
    nbat,
    nrow,
    frames,
    crop_sizes,
    kernel,
    gate_bias,
    peepholes,
    cotangent,
    kernel_first,
    kernel_second,
    bias_first,
    bias_second,
    peep_first,
    peep_second,
):
    frames_n, rows_n = frames.shape[1], frames.shape[3]
    pix = rows_n * WID
    own = kernel.shape[1]
    nlow = max(1, UNIT // own)
    ncore = 2 if nrow > nlow else 1
    nmid = 2 * (nrow // (nlow * ncore))
    nfar = nbat // 2
    at_r = lax.axis_index("rows")

    kt = kernel.T
    if nlow > 1:
        kt = lax.dynamic_update_slice(
            jnp.zeros((UNIT, KROWS), F32), kt, (lax.rem(at_r, nlow) * own, 0)
        )
    bias_row = gate_bias.reshape(1, own)

    vm = pltpu.VMEM
    part = (UNIT, PART)
    pair = (nfar, nmid) if ncore > 1 else (1, 1)
    acc_shapes = [
        [vm((nfar, nmid, ncore) + part, F32), vm(pair + part, F32)] for _ in range(3)
    ]
    ncopies = (
        3 * (nfar + nmid + ncore + nlow - 4)
        + 4 * (nfar + nmid + ncore - 3)
        + 3 * (nfar + nmid + ncore - 3)
        + 4
        + 4 * (frames_n - 1)
        + 2 * (nlow - 1)
    )
    scratch = [
        vm((nfar, nmid, ncore, UNIT, KALL), BF16),
        vm((FPAD, GATES), BF16),
        vm((frames_n, rows_n + 2, CIN, WID), F32),
        vm((frames_n, WIDE + FEAT, (rows_n + 2) * WID), BF16),
        vm((frames_n - 1, rows_n + 2, WID, WIDE), BF16),
        vm((frames_n, pix, GATES), F32),
        vm((frames_n, pix, HID), F32),
        vm((frames_n, pix, GATES), BF16),
        vm((rows_n + 2, WID, HID), F32),
        vm((frames_n, rows_n, WID, HID), BF16),
        vm((WID, HID), F32),
        vm((8, HID), F32),
        vm((7, 8, HID), F32),
        acc_shapes,
        vm((9 * CIN, GATES), F32),
        vm((frames_n, CIN, rows_n, WID), F32),
        vm((2, frames_n, CIN, WID), BF16),
        vm((2, frames_n, CIN, WID), BF16),
        vm((frames_n - 1, 2, WID, HID), BF16),
        vm((frames_n - 1, 2, WID, HID), BF16),
        vm((frames_n - 1, 2, WID, HID), BF16),
        vm((2, frames_n, CIN, WID), BF16),
        vm((2, frames_n, CIN, WID), BF16),
        vm((UNIT, KALL), F32),
    ]
    scratch += [vm(pair + part, BF16)] * 6
    scratch += [vm((nmid - 1, nfar) + part, BF16)] * 6
    scratch += [vm((nfar,) + part, BF16)] * 3 + [vm((nfar - 1,) + part, BF16)] * 3
    scratch += [vm((3, size, 8, HID), F32) for size in (nfar, nmid, ncore, nlow)]
    scratch += [vm((UNIT, KALL), BF16), vm((2, max(1, nlow - 1), UNIT, KALL), BF16)]
    scratch += [
        pltpu.SemaphoreType.DMA((ncopies,)),
        pltpu.SemaphoreType.DMA((ncopies,)),
        pltpu.SemaphoreType.DMA((2 + frames_n,)),
    ]
    smem = pl.BlockSpec(memory_space=pltpu.SMEM)
    vmem = pl.BlockSpec(memory_space=pltpu.VMEM)
    hbm = pl.BlockSpec(memory_space=pl.ANY)
    dims = (nbat, nrow, frames_n, rows_n, nfar, nmid, ncore, nlow)
    hidden, frames_back, kernel_sum, small_sum, norm = pl.pallas_call(
        functools.partial(layer_kernel, dims),
        out_shape=(
            jax.ShapeDtypeStruct(cotangent.shape, BF16),
            jax.ShapeDtypeStruct(frames.shape, F32),
            jax.ShapeDtypeStruct((UNIT, KROWS), F32),
            jax.ShapeDtypeStruct((8, HID), F32),
            jax.ShapeDtypeStruct((8, HID), F32),
        ),
        in_specs=[smem, vmem, vmem, vmem, vmem, hbm],
        out_specs=(hbm, hbm, vmem, vmem, vmem),
        scratch_shapes=scratch,
        compiler_params=pltpu.CompilerParams(
            collective_id=0, has_side_effects=True, vmem_limit_bytes=63 << 20
        ),
        name="layer",
    )(crop_sizes, frames, kt, bias_row, peepholes, cotangent)

    if nlow > 1:
        kernel_sum = lax.dynamic_slice_in_dim(kernel_sum, lax.rem(at_r, nlow) * own, own, 0)
    kshape = jax.ShapeDtypeStruct((own, KROWS), F32)
    bshape = jax.ShapeDtypeStruct((1, own), F32)
    pshape = jax.ShapeDtypeStruct(peepholes.shape, F32)
    outs = pl.pallas_call(
        functools.partial(update_kernel, (nbat, nrow)),
        out_shape=(
            jax.ShapeDtypeStruct(cotangent.shape, BF16),
            jax.ShapeDtypeStruct(frames.shape, F32),
            jax.ShapeDtypeStruct((1, 1), F32),
        )
        + (kshape,) * 3 + (bshape,) * 3 + (pshape,) * 3,
        in_specs=[hbm, hbm, smem] + [vmem] * 11,
        out_specs=(hbm, hbm, smem) + (vmem,) * 9,
        scratch_shapes=[
            pltpu.VMEM(cotangent.shape[1:], BF16),
            pltpu.VMEM(frames.shape[1:], F32),
            pltpu.SemaphoreType.DMA((4, frames_n)),
        ],
        compiler_params=pltpu.CompilerParams(vmem_limit_bytes=63 << 20),
        name="update",
    )(
        hidden, frames_back, norm, kernel_sum, small_sum,
        kernel.T, bias_row, peepholes, kernel_first.T, kernel_second.T,
        bias_first.reshape(1, own), bias_second.reshape(1, own), peep_first, peep_second,
    )
    hidden_seq, frames_grad, norm = outs[:3]
    kernels, biases, peeps = outs[3:6], outs[6:9], outs[9:]
    return (
        hidden_seq,
        frames_grad,
        norm[0, 0],
        *(k.T for k in kernels),
        *(v.reshape(own) for v in biases),
        *peeps,
    )


def solution(mesh):
    return jax.shard_map(
        functools.partial(local, mesh.shape["batch"], mesh.shape["rows"]),
        mesh=mesh,
        in_specs=(
            P("batch", None, None, "rows", None),
            P("batch", None),
            P(None, ("batch", "rows")),
            P(("batch", "rows")),
            P(None, "batch"),
            P("batch", None, "rows", None, None),
            P(None, ("batch", "rows")),
            P(None, ("batch", "rows")),
            P(("batch", "rows")),
            P(("batch", "rows")),
            P(None, "batch"),
            P(None, "batch"),
        ),
        out_specs=(
            P("batch", None, "rows", None, None),
            P("batch", None, None, "rows", None),
            P(),
            P(None, ("batch", "rows")),
            P(None, ("batch", "rows")),
            P(None, ("batch", "rows")),
            P(("batch", "rows")),
            P(("batch", "rows")),
            P(("batch", "rows")),
            P(None, "batch"),
            P(None, "batch"),
            P(None, "batch"),
        ),
        check_vma=False,
    )
```

time: 131 us -> 107 us (0.82)
  Pallas kernels: 117 us -> 106 us
  local copies, waits for them, and re-layouts: 7.01 us -> 0 us
  other arithmetic: 5 us -> 0 us
    pallas_call x1, Pallas kernels: 117 us -> 101 us  [local(): pl.pallas_call(functools.partial(layer_kernel, dims), out_shape=(jax.Shap...]
    pallas_call x0 -> x1, Pallas kernels: none -> 4.52 us  [local(): pl.pallas_call(functools.partial(update_kernel, (nbat, nrow)), out_shape=...]
    unnamed x22 -> x0, local copies, waits for them, and re-layouts: 4.06 us -> none
    sub x3 -> x0, other arithmetic: 3.6 us -> none  [adamw_update(): weight - LEARN_RATE * (first_hat / (jnp.sqrt(second_hat) + ADAM_EPS) + WE...]
where the time goes in v2:
time: 107 us; the launch traced here: 106 us
  Pallas kernels  106 us (99%)
    pallas_call x1, Pallas kernels, local(): pl.pallas_call(functools.partial(layer_kernel, dims), out_shape=(jax.Shap...  101 us
    pallas_call x1, Pallas kernels, local(): pl.pallas_call(functools.partial(update_kernel, (nbat, nrow)), out_shape=...  4.52 us

profile of v2, /device:TPU:0, one launch (start us, length us, event | category | flops | bytes accessed | tf_op | source)
XLA Modules:
  0.0 106.5 jit_solution(14628127681128484776)
XLA Ops:
  0.6 101.2 %layer.1 = (bf16[1,4,16,128,128]{4,3,2,1,0:T(8,128)(2,1)}, f32[1,4,16,16,128]{4,3,2,1,0:T(8,128)}, f32[16,1296]{1,0:T(8,128)}, f32[8,128]{1,0:T(8,128)}, f32[8,128]{1,0:T(8,128)}) custom-call(s32[1,2]{1,0:T(1,128)} %crop_ref.1, bf16[1,4,16,16,128]{4,3,2,1,0:T(8,128)(2,1)} %frames_ref.1, f32[16,1296]{1,0:T(8,128)} %bitcast.13, f32[1,16]{1,0:T(1,128)} %bitcast.17, ...), custom_call_target="tpu_custom_call" | custom-call | tf_op jit(solution)/shard_map/layer/pallas_call | solution.py:801
  101.8 4.5 %update.1 = (bf16[1,4,16,128,128]{4,3,2,1,0:T(8,128)(2,1)}, f32[1,4,16,16,128]{4,3,2,1,0:T(8,128)}, f32[1,1]{1,0:T(1,128)}, f32[16,1296]{1,0:T(8,128)}, f32[16,1...) custom-call(bf16[1,4,16,128,128]{4,3,2,1,0:T(8,128)(2,1)} %get-tuple, ...), custom_call_target="tpu_custom_call" | custom-call | tf_op jit(solution)/shard_map/update/pallas_call | solution.py:824

commit v3 on v2

--- a/solution.py
+++ b/solution.py
@@ -61,13 +61,13 @@
     wft,
     fr,
     xt,
+    xt0,
     sc,
     gates,
     cells,
     gpre,
     gs,
     cot,
-    srow,
     consts,
     sums,
     acc,
@@ -91,6 +91,7 @@
     )
     small_bufs = [rest.pop(0) for _ in range(4)]
     low_send, low_recv = rest.pop(0), rest.pop(0)
+    norm_tiles, nsems = rest.pop(0), rest.pop(0)
     sems = rest.pop(0)
     rsems = rest.pop(0)
     lsems = rest.pop(0)
@@ -137,13 +138,18 @@
     down_r = lax.rem(at_r + 1, nrow)
 
     barrier = pltpu.get_barrier_semaphore()
-    greeted = 2
-    pl.semaphore_signal(barrier, inc=1, device_id=(at_b, up_r), device_id_type=MESH)
-    pl.semaphore_signal(barrier, inc=1, device_id=(at_b, down_r), device_id_type=MESH)
-    for size, peer, _ in groups:
-        for k in range(1, size):
-            pl.semaphore_signal(barrier, inc=1, device_id=peer(k), device_id_type=MESH)
-            greeted += 1
+    ndev = nbat * nrow
+    me = at_b * nrow + at_r
+
+    def any_peer(k):
+        to = lax.rem(me + k, ndev)
+        return (to // nrow, lax.rem(to, nrow))
+
+    def greet(k, carry):
+        pl.semaphore_signal(barrier, inc=1, device_id=any_peer(k), device_id_type=MESH)
+        return carry
+
+    lax.fori_loop(1, ndev, greet, 0)
 
     cot_copy = pltpu.make_async_copy(cot_hbm.at[0], cot, lsems.at[0])
     cot_copy.start()
@@ -169,9 +175,8 @@
     bias_tile = jnp.where(tile_row == 4 + flat // HID, bias_tile, 0.0)
     start_tile = jnp.where(at_r == 0, peep_tile, 0.0) + bias_tile
 
-    small_step = [0] * 3
-    small_sum = [None] * 3
-    small_moving = [None] * 3
+    small_step = [0] * 2
+    small_moving = [None] * 2
 
     def small_next(i, tile=None):
         s = small_step[i]
@@ -261,10 +266,13 @@
             return jnp.where(at == WID - 1, 0.0, pltpu.roll(v, WID - 1, 0))
         return jnp.where(at == 0, 0.0, pltpu.roll(v, 1, 0))
 
+    def frame_part(t):
+        return xt.at[t - 1, WIDE : WIDE + FEAT] if t > 0 else xt0
+
     def frame_cols(t, rr):
         v = fr[t, rr]
         three = jnp.concatenate([lane_shift(v, -1), v, lane_shift(v, 1)], axis=0)
-        xt[t, WIDE : WIDE + FEAT, pl.ds(pl.multiple_of(rr * WID, WID), WID)] = three.astype(BF16)
+        frame_part(t)[:, pl.ds(pl.multiple_of(rr * WID, WID), WID)] = three.astype(BF16)
 
     def frame_cols_all(rr, carry):
         for t in range(frames_n):
@@ -274,7 +282,7 @@
     def frame_pixels(t, lo, up):
         def one(rr, carry):
             parts = [
-                xt[t, WIDE : WIDE + FEAT, pl.ds(pl.multiple_of((rr + a) * WID, WID), WID)].astype(F32)
+                frame_part(t)[:, pl.ds(pl.multiple_of((rr + a) * WID, WID), WID)].astype(F32)
                 for a in range(3)
             ]
             parts.append(jnp.zeros((FPAD - 9 * CIN, WID), F32))
@@ -288,7 +296,7 @@
     lax.fori_loop(1, rows_n + 1, frame_cols_all, 0)
     frame_pixels(0, 1, rows_n - 1)
 
-    pl.semaphore_wait(barrier, greeted)
+    pl.semaphore_wait(barrier, ndev - 1)
     gather_low()
     gather_step(0)
     small_next(0, start_tile)
@@ -337,97 +345,93 @@
     def place_state(t, v, at):
         three = [row_shift(v, -1), v, row_shift(v, 1)]
         for j in range(3):
-            sc[t, at, :, j * HID : (j + 1) * HID] = three[j].astype(BF16)
-        vt = v.T
-        three = [lane_shift(vt, -1), vt, lane_shift(vt, 1)]
-        for j in range(3):
-            xt[t + 1, j * HID : (j + 1) * HID, pl.ds(pl.multiple_of(at * WID, WID), WID)] = three[j].astype(BF16)
-
-    def forward_row(t, rr):
-        limit = live_cols(rr)
-        for j in range(WID // SUB):
-            sl = pl.ds(pl.multiple_of(rr * WID + j * SUB, SUB), SUB)
-            live = sub_iota + j * SUB < limit
-            zi = gates[t, sl, 0:HID] + bias[0]
-            zc = gates[t, sl, 2 * HID : 3 * HID] + bias[2]
-            zo = gates[t, sl, 3 * HID :] + bias[3]
-            if t > 0:
-                prev = cells[t - 1, sl, :]
-                zf = gates[t, sl, HID : 2 * HID] + bias[1] + peep[1] * prev
-                zi = zi + peep[0] * prev
-                gf = sigmoid(zf)
-                gates[t, sl, HID : 2 * HID] = gf
-            gi = sigmoid(zi)
-            gc = jnp.tanh(zc)
-            c = gi * gc
-            if t > 0:
-                c = c + gf * prev
-            c = jnp.where(live, c, 0.0)
-            go = sigmoid(zo + peep[2] * c)
-            gates[t, sl, 0:HID] = gi
-            gates[t, sl, 2 * HID : 3 * HID] = gc
-            gates[t, sl, 3 * HID :] = go
-            cells[t, sl, :] = c
-            srow[j * SUB : (j + 1) * SUB, :] = jnp.where(live, go * jnp.tanh(c), 0.0)
-        if t < frames_n - 1:
-            place_state(t, srow[...], rr + 1)
-        else:
-            sc[0, rr + 1, :, 0:HID] = srow[...].astype(BF16)
+            low_j = three[j].astype(BF16)
+            sc[t, at, :, j * HID : (j + 1) * HID] = low_j
+            xt[t, j * HID : (j + 1) * HID, at * WID : (at + 1) * WID] = low_j.T
 
     CH = 4
-
-    def forward_chunk(t, m):
-        px = pl.ds(pl.multiple_of(m * CH * WID, CH * WID), CH * WID)
+    nchunk = rows_n // CH
+
+    def forward_dot(t, m):
+        px = pl.ds(m * CH * WID, CH * WID)
         xf = gpre[t, px, 0:FPAD]
         if t > 0:
-            parts = [
-                sc[t - 1, pl.ds(m * CH + a, CH)].reshape(CH * WID, WIDE) for a in range(3)
-            ]
+            parts = [sc[t - 1, m * CH + a : m * CH + a + CH].reshape(CH * WID, WIDE) for a in range(3)]
             x = jnp.concatenate(parts + [xf], axis=1)
             gates[t, px, :] = mm(x, cat_wt(0, KALL), NT)
         else:
             gates[t, px, :] = mm(xf, cat_wt(HALL, KALL), NT)
 
-        def one(i, carry):
-            forward_row(t, m * CH + i)
-            return carry
-
-        lax.fori_loop(0, CH, one, 0)
-
-    nchunk = rows_n // CH
+    def forward_rows(t, m):
+        for rr in range(m * CH, (m + 1) * CH):
+            limit = live_cols(rr)
+            state = []
+            for j in range(WID // SUB):
+                sl = pl.ds(rr * WID + j * SUB, SUB)
+                live = sub_iota + j * SUB < limit
+                zi = gates[t, sl, 0:HID] + bias[0]
+                zc = gates[t, sl, 2 * HID : 3 * HID] + bias[2]
+                zo = gates[t, sl, 3 * HID :] + bias[3]
+                if t > 0:
+                    prev = cells[t - 1, sl, :]
+                    zf = gates[t, sl, HID : 2 * HID] + bias[1] + peep[1] * prev
+                    zi = zi + peep[0] * prev
+                    gf = sigmoid(zf)
+                    gates[t, sl, HID : 2 * HID] = gf
+                gi = sigmoid(zi)
+                gc = jnp.tanh(zc)
+                c = gi * gc
+                if t > 0:
+                    c = c + gf * prev
+                c = jnp.where(live, c, 0.0)
+                go = sigmoid(zo + peep[2] * c)
+                gates[t, sl, 0:HID] = gi
+                gates[t, sl, 2 * HID : 3 * HID] = gc
+                gates[t, sl, 3 * HID :] = go
+                cells[t, sl, :] = c
+                state.append(jnp.where(live, go * jnp.tanh(c), 0.0))
+            state = jnp.concatenate(state, axis=0)
+            if t < frames_n - 1:
+                place_state(t, state, rr + 1)
+            else:
+                sc[0, rr + 1, :, 0:HID] = state.astype(BF16)
+
     hid_copies = []
-    halo = None
-    for t in range(frames_n):
-        if t == 0:
-            for m in range(nchunk):
-                forward_chunk(0, m)
-                if m < 3:
-                    gather_step(1 + m)
-            for i in range(1, 4):
-                while steps[i] < 4:
-                    gather_step(i)
-        else:
-            lax.fori_loop(1, nchunk - 1, lambda m, c: (forward_chunk(t, m), c)[1], 0)
-        if halo is not None:
-            halo[0].wait_recv()
-            halo[1].wait_recv()
+    center = pl.ds(HID, HID)
+    halos = [[None, None] for _ in range(frames_n)]
+
+    def state_done(t, m):
+        if t < frames_n - 1 and m == 0:
+            halos[t][1] = remote(sc.at[t, 1, :, center], shalo_r.at[t, 1], at_b, up_r)
+        if t < frames_n - 1 and m == nchunk - 1:
+            halos[t][0] = remote(sc.at[t, rows_n, :, center], shalo_r.at[t, 0], at_b, down_r)
+        if (t, m) == last_of[t]:
+            lanes_of = center if t < frames_n - 1 else pl.ds(0, HID)
+            src = sc.at[t if t < frames_n - 1 else 0, pl.ds(1, rows_n), :, lanes_of]
+            c = pltpu.make_async_copy(src, hid_hbm.at[0, t], lsems.at[1 + t])
+            c.start()
+            hid_copies.append(c)
+
+    order = list(range(1, nchunk - 1)) + [0, nchunk - 1]
+    slots = [(0, m) for m in range(nchunk)] + [(t, m) for t in range(1, frames_n) for m in order]
+    last_of = {t: [s for s in slots if s[0] == t][-1] for t in range(frames_n)}
+    for i, (t, m) in enumerate(slots + [(frames_n, 0)]):
+        if t == 1 and m == order[0]:
+            for k in range(1, 4):
+                while steps[k] < 4:
+                    gather_step(k)
+        if 0 < t < frames_n and m == order[nchunk - 2]:
+            for k in range(2):
+                halos[t - 1][k].wait_recv()
             place_state(t - 1, shalo_r[t - 1, 0].astype(F32) * has_up, 0)
             place_state(t - 1, shalo_r[t - 1, 1].astype(F32) * has_down, rows_n + 1)
-        if t > 0:
-            lax.fori_loop(0, 2, lambda m, c: (forward_chunk(t, m * (nchunk - 1)), c)[1], 0)
-        if t < frames_n - 1:
-            center = pl.ds(HID, HID)
-            halo = (
-                remote(sc.at[t, 1, :, center], shalo_r.at[t, 1], at_b, up_r),
-                remote(sc.at[t, rows_n, :, center], shalo_r.at[t, 0], at_b, down_r),
-            )
-            c = pltpu.make_async_copy(sc.at[t, pl.ds(1, rows_n), :, center], hid_hbm.at[0, t], lsems.at[1 + t])
-        else:
-            c = pltpu.make_async_copy(
-                sc.at[0, pl.ds(1, rows_n), :, pl.ds(0, HID)], hid_hbm.at[0, t], lsems.at[1 + t]
-            )
-        c.start()
-        hid_copies.append(c)
+        if t < frames_n:
+            forward_dot(t, m)
+        if i > 0:
+            forward_rows(*slots[i - 1])
+            state_done(*slots[i - 1])
+        if t == 0 and 0 < m < 4:
+            gather_step(m)
 
     cot_copy.wait()
     sums[...] = jnp.zeros_like(sums)
@@ -435,96 +439,93 @@
     def fold(v):
         return jnp.sum(v.reshape(SUB // 8, 8, HID), axis=0)
 
-    def backward_row(t, rr):
-        limit = live_cols(rr)
+    def backward_rows(t, m):
         parts = [None] * 7
-        for j in range(WID // SUB):
-            sl = pl.ds(pl.multiple_of(rr * WID + j * SUB, SUB), SUB)
-            live = sub_iota + j * SUB < limit
-            gi = gates[t, sl, 0:HID]
-            gc = gates[t, sl, 2 * HID : 3 * HID]
-            go = gates[t, sl, 3 * HID :]
-            c = cells[t, sl, :]
-            sq = jnp.tanh(c)
-            total = cot[t, rr, j * SUB : (j + 1) * SUB, :].astype(F32)
-            if t < frames_n - 1:
-                total = total + gs[rr + 1, j * SUB : (j + 1) * SUB, :]
-            total = jnp.where(live, total, 0.0)
-            tgo = total * go
-            d_out = tgo * sq * (1.0 - go)
-            nxt = tgo * (1.0 - sq * sq) + peep[2] * d_out
-            if t < frames_n - 1:
-                nxt = nxt + cells[t + 1, sl, :]
-            kept = jnp.where(live, nxt, 0.0)
-            kgi = kept * gi
-            d_in = kgi * gc * (1.0 - gi)
-            d_cand = kgi * (1.0 - gc * gc)
-            vals = [d_in, None, d_cand, d_out, None, None, d_out * c]
-            if t > 0:
-                gf = gates[t, sl, HID : 2 * HID]
-                prev = cells[t - 1, sl, :]
-                kgf = kept * gf
-                d_for = kgf * prev * (1.0 - gf)
-                cells[t, sl, :] = kgf + peep[0] * d_in + peep[1] * d_for
-                vals[1] = d_for
-                vals[4] = d_in * prev
-                vals[5] = d_for * prev
-            gpre[t, sl, 0:HID] = d_in.astype(BF16)
-            gpre[t, sl, HID : 2 * HID] = (vals[1] if t > 0 else jnp.zeros_like(d_in)).astype(BF16)
-            gpre[t, sl, 2 * HID : 3 * HID] = d_cand.astype(BF16)
-            gpre[t, sl, 3 * HID :] = d_out.astype(BF16)
-            for i in range(7):
-                if vals[i] is not None:
-                    f = fold(vals[i])
-                    parts[i] = f if parts[i] is None else parts[i] + f
+        for rr in range(m * CH, (m + 1) * CH):
+            limit = live_cols(rr)
+            for j in range(WID // SUB):
+                cols = slice(j * SUB, (j + 1) * SUB)
+                sl = pl.ds(rr * WID + j * SUB, SUB)
+                live = sub_iota + j * SUB < limit
+                gi = gates[t, sl, 0:HID]
+                gc = gates[t, sl, 2 * HID : 3 * HID]
+                go = gates[t, sl, 3 * HID :]
+                c = cells[t, sl, :]
+                sq = jnp.tanh(c)
+                total = cot[t, rr, cols, :].astype(F32)
+                if t < frames_n - 1:
+                    total = total + gs[(t + 1) % 2, rr + 1, cols, :]
+                    if rr == 0:
+                        total = total + ghalo_r[t, 0, cols, :].astype(F32) * has_up
+                    if rr == rows_n - 1:
+                        total = total + ghalo_r[t, 1, cols, :].astype(F32) * has_down
+                total = jnp.where(live, total, 0.0)
+                tgo = total * go
+                d_out = tgo * sq * (1.0 - go)
+                nxt = tgo * (1.0 - sq * sq) + peep[2] * d_out
+                if t < frames_n - 1:
+                    nxt = nxt + cells[t + 1, sl, :]
+                kept = jnp.where(live, nxt, 0.0)
+                kgi = kept * gi
+                d_in = kgi * gc * (1.0 - gi)
+                d_cand = kgi * (1.0 - gc * gc)
+                vals = [d_in, None, d_cand, d_out, None, None, d_out * c]
+                if t > 0:
+                    gf = gates[t, sl, HID : 2 * HID]
+                    prev = cells[t - 1, sl, :]
+                    kgf = kept * gf
+                    d_for = kgf * prev * (1.0 - gf)
+                    cells[t, sl, :] = kgf + peep[0] * d_in + peep[1] * d_for
+                    vals[1] = d_for
+                    vals[4] = d_in * prev
+                    vals[5] = d_for * prev
+                gpre[t, sl, 0:HID] = d_in.astype(BF16)
+                gpre[t, sl, HID : 2 * HID] = (vals[1] if t > 0 else jnp.zeros_like(d_in)).astype(BF16)
+                gpre[t, sl, 2 * HID : 3 * HID] = d_cand.astype(BF16)
+                gpre[t, sl, 3 * HID :] = d_out.astype(BF16)
+                for i in range(7):
+                    if vals[i] is not None:
+                        f = fold(vals[i])
+                        parts[i] = f if parts[i] is None else parts[i] + f
         for i in range(7):
             if parts[i] is not None:
                 sums[i] = sums[i] + parts[i]
 
-    def state_chunk(t, m):
-        px = pl.ds(pl.multiple_of(m * CH * WID, CH * WID), CH * WID)
-        y = mm(gpre[t, px, :], cat_wt(0, HALL), NN)
-        for a in range(3):
-            buf = acc[a][0]
-            buf[..., 0:WIDE] = y[:, a * WIDE : (a + 1) * WIDE].reshape(buf.shape[:-1] + (WIDE,))
-
-        def one(i, carry):
+    def state_chunk(t, m, done):
+        y = mm(gpre[t, m * CH * WID : (m + 1) * CH * WID, :], cat_wt(0, HALL), NN)
+        row = [None] * (CH + 2)
+        for i in range(CH):
             for a in range(3):
-                buf = acc[a][0]
-                per = nfar // CH
-                three = [
-                    buf[pl.ds(i * per, per), :, :, :, j * HID : (j + 1) * HID].reshape(WID, HID)
-                    for j in range(3)
-                ]
+                three = [y[i * WID : (i + 1) * WID, a * WIDE + j * HID : a * WIDE + (j + 1) * HID] for j in range(3)]
                 z = three[1] + row_shift(three[0], 1) + row_shift(three[2], -1)
-                at = m * CH + i + a
-                gs[at] = gs[at] + z
-            return carry
-
-        lax.fori_loop(0, CH, one, 0)
-
-    halo = None
-    for t in reversed(range(frames_n)):
-        lax.fori_loop(1, rows_n - 1, lambda rr, c: (backward_row(t, rr), c)[1], 0)
-        if halo is not None:
-            halo[0].wait_recv()
-            halo[1].wait_recv()
-            gs[1] = gs[1] + ghalo_r[t, 0].astype(F32) * has_up
-            gs[rows_n] = gs[rows_n] + ghalo_r[t, 1].astype(F32) * has_down
-        lax.fori_loop(0, 2, lambda k, c: (backward_row(t, k * (rows_n - 1)), c)[1], 0)
-        if t > 0:
-            gs[...] = jnp.zeros_like(gs)
-            lax.fori_loop(0, 2, lambda k, c: (state_chunk(t, k * (nchunk - 1)), c)[1], 0)
-            ghalo_s[t - 1, 0] = gs[0].astype(BF16)
-            ghalo_s[t - 1, 1] = gs[rows_n + 1].astype(BF16)
-            halo = (
-                remote(ghalo_s.at[t - 1, 0], ghalo_r.at[t - 1, 1], at_b, up_r),
-                remote(ghalo_s.at[t - 1, 1], ghalo_r.at[t - 1, 0], at_b, down_r),
-            )
-            lax.fori_loop(1, nchunk - 1, lambda m, c: (state_chunk(t, m), c)[1], 0)
-
-    rows = [jnp.sum(sums[i], axis=0, keepdims=True) for i in range(7)]
-    small_next(1, jnp.concatenate(rows[4:] + [jnp.zeros((1, HID), F32)] + rows[:4], axis=0))
+                row[i + a] = z if row[i + a] is None else row[i + a] + z
+        for k in range(CH + 2):
+            at = m * CH + k
+            gs[t % 2, at] = gs[t % 2, at] + row[k] if at in done else row[k]
+            done.add(at)
+
+    work = [(t, m) for t in reversed(range(frames_n)) for m in order]
+    backward_rows(*work[0])
+    ghalos = [[None, None] for _ in range(frames_n)]
+
+    def rows_ready(t, m):
+        if t < frames_n - 1 and m in (0, nchunk - 1):
+            ghalos[t + 1][0 if m == 0 else 1].wait_recv()
+
+    written = {t: set() for t in range(frames_n)}
+    for i, (t, m) in enumerate(work):
+        if t == 0:
+            break
+        rows_ready(*work[i + 1])
+        state_chunk(t, m, written[t])
+        backward_rows(*work[i + 1])
+        if m == 0:
+            ghalo_s[t - 1, 0] = gs[t % 2, 0].astype(BF16)
+            ghalos[t][1] = remote(ghalo_s.at[t - 1, 0], ghalo_r.at[t - 1, 1], at_b, up_r)
+        if m == nchunk - 1:
+            ghalo_s[t - 1, 1] = gs[t % 2, rows_n + 1].astype(BF16)
+            ghalos[t][0] = remote(ghalo_s.at[t - 1, 1], ghalo_r.at[t - 1, 0], at_b, down_r)
+    left = work[-(nchunk - 1) :]
 
     stage = [0] * 3
     flight = [None] * 3
@@ -567,23 +568,42 @@
                 nat[:, at : at + CIN] = total[:, WIDE + j * CIN : WIDE + (j + 1) * CIN]
                 nat[:, at + CIN : at + CIN + HID] = total[:, j * HID : (j + 1) * HID]
 
-    g0 = [xt[0, WIDE : WIDE + FEAT, a * WID : a * WID + pix] for a in range(3)]
-    fzero[...] = mm(jnp.concatenate(g0, axis=0), gpre[0], NN)
-
+    def kernel_dot(a, t):
+        return mm(xt[t - 1, :, a * WID : a * WID + pix], gpre[t], NN)
+
+    def finish_rows(k):
+        rows_ready(*left[k])
+        backward_rows(*left[k])
+
+    def place_chunk(a, total):
+        extra = total[WIDE:, :] + fzero[a * FEAT : (a + 1) * FEAT, :]
+        whole = jnp.concatenate([total[:WIDE, :], extra, jnp.zeros((PART - WIDE - FEAT, GATES), F32)], axis=0)
+        acc[a][0][...] = whole.T.reshape(acc[a][0].shape)
+
+    totals = [None] * 3
     for a in range(3):
-        total = None
         for t in range(1, frames_n):
-            part = mm(xt[t, :, a * WID : a * WID + pix], gpre[t], NN)
-            total = part if total is None else total + part
-            if t == 1 and a > 0:
+            part = kernel_dot(a, t)
+            totals[a] = part if t == 1 else totals[a] + part
+            if a == 0 and t - 1 < len(left):
+                finish_rows(t - 1)
+            if a > 0 and t == 1:
+                place_chunk(a - 1, totals[a - 1])
+                reduce_step(a - 1)
+            if a > 0 and t == 2:
                 if a > 1:
                     reduce_step(a - 2)
                 reduce_step(a - 1)
                 small_next(1)
-        extra = total[WIDE:, :] + fzero[a * FEAT : (a + 1) * FEAT, :]
-        whole = jnp.concatenate([total[:WIDE, :], extra, jnp.zeros((PART - WIDE - FEAT, GATES), F32)], axis=0)
-        acc[a][0][...] = whole.T.reshape(acc[a][0].shape)
-        reduce_step(a)
+        if a == 0:
+            for k in range(frames_n - 1, len(left)):
+                finish_rows(k)
+            g0 = [xt0[:, k * WID : k * WID + pix] for k in range(3)]
+            fzero[...] = mm(jnp.concatenate(g0, axis=0), gpre[0], NN)
+            rows = [jnp.sum(sums[i], axis=0, keepdims=True) for i in range(7)]
+            small_next(1, jnp.concatenate(rows[4:] + [jnp.zeros((1, HID), F32)] + rows[:4], axis=0))
+    place_chunk(2, totals[2])
+    reduce_step(2)
 
     fgb = fr
 
@@ -636,13 +656,21 @@
         base = low * rows_own
         ri = lax.broadcasted_iota(jnp.int32, squares.shape, 0)
         squares = jnp.where((ri >= base) & (ri < base + rows_own), squares, 0.0)
-    small_next(2, jnp.broadcast_to(jnp.sum(squares), (8, HID)))
+    norm_tiles[me] = jnp.broadcast_to(jnp.sum(squares), (8, HID))
+
+    def norm_copy(k):
+        row = norm_tiles.at[me, 0:1]
+        return pltpu.make_async_remote_copy(
+            src_ref=row, dst_ref=row, send_sem=nsems.at[0, k], recv_sem=nsems.at[1, k],
+            device_id=any_peer(k), device_id_type=MESH,
+        )
+
+    lax.fori_loop(1, ndev, lambda k, c: (norm_copy(k).start(), c)[1], 0)
     grad_ref[...] = g
     small = small_finish(1)
     small_out[...] = small
     f_up.wait_recv()
     f_down.wait_recv()
-    small_next(2)
     for t in range(frames_n):
         fgb[t, 1] = fgb[t, 1] + bhalo_r[0, t].astype(F32) * has_up
         fgb[t, rows_n] = fgb[t, rows_n] + bhalo_r[1, t].astype(F32) * has_down
@@ -650,8 +678,10 @@
     c = pltpu.make_async_copy(fgo, fg_hbm.at[0], lsems.at[1 + frames_n])
     c.start()
     hid_copies.append(c)
-    squares = small_finish(2) + jnp.sum(small * small)
-    norm_out[...] = jnp.sqrt(squares)
+    lax.fori_loop(1, ndev, lambda k, c: (norm_copy(k).wait_recv(), c)[1], 0)
+    squares = jnp.sum(norm_tiles[:, 0:1, :], axis=0) + jnp.sum(small * small)
+    norm_out[...] = jnp.broadcast_to(jnp.sqrt(squares), (8, HID))
+    lax.fori_loop(1, ndev, lambda k, c: (norm_copy(k).wait_send(), c)[1], 0)
 
     for c in hid_copies:
         c.wait()
@@ -751,7 +781,7 @@
         [vm((nfar, nmid, ncore) + part, F32), vm(pair + part, F32)] for _ in range(3)
     ]
     ncopies = (
-        3 * (nfar + nmid + ncore + nlow - 4)
+        2 * (nfar + nmid + ncore + nlow - 4)
         + 4 * (nfar + nmid + ncore - 3)
         + 3 * (nfar + nmid + ncore - 3)
         + 4
@@ -762,14 +792,14 @@
         vm((nfar, nmid, ncore, UNIT, KALL), BF16),
         vm((FPAD, GATES), BF16),
         vm((frames_n, rows_n + 2, CIN, WID), F32),
-        vm((frames_n, WIDE + FEAT, (rows_n + 2) * WID), BF16),
+        vm((frames_n - 1, WIDE + FEAT, (rows_n + 2) * WID), BF16),
+        vm((FEAT, (rows_n + 2) * WID), BF16),
         vm((frames_n - 1, rows_n + 2, WID, WIDE), BF16),
         vm((frames_n, pix, GATES), F32),
         vm((frames_n, pix, HID), F32),
         vm((frames_n, pix, GATES), BF16),
-        vm((rows_n + 2, WID, HID), F32),
+        vm((2, rows_n + 2, WID, HID), F32),
         vm((frames_n, rows_n, WID, HID), BF16),
-        vm((WID, HID), F32),
         vm((8, HID), F32),
         vm((7, 8, HID), F32),
         acc_shapes,
@@ -787,8 +817,9 @@
     scratch += [vm(pair + part, BF16)] * 6
     scratch += [vm((nmid - 1, nfar) + part, BF16)] * 6
     scratch += [vm((nfar,) + part, BF16)] * 3 + [vm((nfar - 1,) + part, BF16)] * 3
-    scratch += [vm((3, size, 8, HID), F32) for size in (nfar, nmid, ncore, nlow)]
+    scratch += [vm((2, size, 8, HID), F32) for size in (nfar, nmid, ncore, nlow)]
     scratch += [vm((UNIT, KALL), BF16), vm((2, max(1, nlow - 1), UNIT, KALL), BF16)]
+    scratch += [vm((nbat * nrow, 8, HID), F32), pltpu.SemaphoreType.DMA((2, nbat * nrow))]
     scratch += [
         pltpu.SemaphoreType.DMA((ncopies,)),
         pltpu.SemaphoreType.DMA((ncopies,)),

time: 107 us -> 88.6 us (0.83)
  Pallas kernels: 106 us -> 87.5 us
    pallas_call x1, Pallas kernels: 101 us -> 83 us  [local(): pl.pallas_call(functools.partial(layer_kernel, dims), out_shape=(jax.Shap...]
where the time goes in v3:
time: 88.6 us; the launch traced here: 88.4 us
  Pallas kernels  87.5 us (99%)
    pallas_call x1, Pallas kernels, local(): pl.pallas_call(functools.partial(layer_kernel, dims), out_shape=(jax.Shap...  83 us
    pallas_call x1, Pallas kernels, local(): pl.pallas_call(functools.partial(update_kernel, (nbat, nrow)), out_shape=...  4.52 us

profile of v3, /device:TPU:0, one launch (start us, length us, event | category | flops | bytes accessed | tf_op | source)
XLA Modules:
  0.0 88.4 jit_solution(14002951962383473049)
XLA Ops:
  0.6 83.0 %layer.1 = (bf16[1,4,16,128,128]{4,3,2,1,0:T(8,128)(2,1)}, f32[1,4,16,16,128]{4,3,2,1,0:T(8,128)}, f32[16,1296]{1,0:T(8,128)}, f32[8,128]{1,0:T(8,128)}, f32[8,128]{1,0:T(8,128)}) custom-call(s32[1,2]{1,0:T(1,128)} %crop_ref.1, bf16[1,4,16,16,128]{4,3,2,1,0:T(8,128)(2,1)} %frames_ref.1, f32[16,1296]{1,0:T(8,128)} %bitcast.13, f32[1,16]{1,0:T(1,128)} %bitcast.17, ...), custom_call_target="tpu_custom_call" | custom-call | tf_op jit(solution)/shard_map/layer/pallas_call | solution.py:832
  83.7 4.5 %update.1 = (bf16[1,4,16,128,128]{4,3,2,1,0:T(8,128)(2,1)}, f32[1,4,16,16,128]{4,3,2,1,0:T(8,128)}, f32[1,1]{1,0:T(1,128)}, f32[16,1296]{1,0:T(8,128)}, f32[16,1...) custom-call(bf16[1,4,16,128,128]{4,3,2,1,0:T(8,128)(2,1)} %get-tuple, ...), custom_call_target="tpu_custom_call" | custom-call | tf_op jit(solution)/shard_map/update/pallas_call | solution.py:855

commit v4 on v3

--- a/solution.py
+++ b/solution.py
@@ -31,7 +31,13 @@
 FEAT = 3 * CIN
 FPAD = 256
 KALL = HALL + FPAD
-PART = 512
+PARTS = [
+    (0, 0, WIDE + FEAT, 512),
+    (1, 0, WIDE + FEAT, 512),
+    (2, 2 * HID, WIDE + FEAT, 256),
+    (2, 0, 2 * HID, 256),
+]
+DIRECT = 3
 SUB = 32
 UNIT = 16
 
@@ -87,9 +93,10 @@
     pix = rows_n * WID
     rest = list(rest)
     core_send, core_recv, mid_send, mid_recv, far_send, far_recv = (
-        [rest.pop(0) for _ in range(3)] for _ in range(6)
+        [rest.pop(0) for _ in PARTS] for _ in range(6)
     )
     small_bufs = [rest.pop(0) for _ in range(4)]
+    tail_send, tail_recv = ([rest.pop(0) for _ in PARTS[DIRECT:]] for _ in range(2))
     low_send, low_recv = rest.pop(0), rest.pop(0)
     norm_tiles, nsems = rest.pop(0), rest.pop(0)
     sems = rest.pop(0)
@@ -145,11 +152,10 @@
         to = lax.rem(me + k, ndev)
         return (to // nrow, lax.rem(to, nrow))
 
-    def greet(k, carry):
-        pl.semaphore_signal(barrier, inc=1, device_id=any_peer(k), device_id_type=MESH)
-        return carry
-
-    lax.fori_loop(1, ndev, greet, 0)
+    partners = [(at_b, up_r), (at_b, down_r)]
+    partners += [peer(k) for size, peer, _ in groups for k in range(1, size)]
+    for to in partners:
+        pl.semaphore_signal(barrier, inc=1, device_id=to, device_id_type=MESH)
 
     cot_copy = pltpu.make_async_copy(cot_hbm.at[0], cot, lsems.at[0])
     cot_copy.start()
@@ -230,11 +236,12 @@
             for c in moving[i]:
                 c.wait_recv()
         if s < 3:
-            size, peer, _ = groups[s]
+            g = (1, 0, 2)[s] if i == 1 else s
+            size, peer, _ = groups[g]
             if s == 0:
                 ref = wt.at[far, mid, core, :, cols]
             elif s == 1:
-                ref = wt.at[:, mid, core, :, cols]
+                ref = wt.at[far, :, core, :, cols] if i == 1 else wt.at[:, mid, core, :, cols]
             else:
                 ref = wt.at[:, :, core, :, cols]
             moving[i] = [remote(ref, ref, *peer(k)) for k in range(1, size)]
@@ -296,19 +303,17 @@
     lax.fori_loop(1, rows_n + 1, frame_cols_all, 0)
     frame_pixels(0, 1, rows_n - 1)
 
-    pl.semaphore_wait(barrier, ndev - 1)
+    pl.semaphore_wait(barrier, len(partners))
     gather_low()
     gather_step(0)
+    gather_step(1)
     small_next(0, start_tile)
     f_up = remote(fhalo_s.at[0], fhalo_r.at[1], at_b, up_r)
     f_down = remote(fhalo_s.at[1], fhalo_r.at[0], at_b, down_r)
-    gather_step(1)
     gather_step(2)
     gather_step(3)
     if frames_n > 1:
         frame_pixels(1, 1, rows_n - 1)
-    gather_step(0)
-    small_next(0)
     f_up.wait_recv()
     f_down.wait_recv()
     for t in range(frames_n):
@@ -316,16 +321,18 @@
         fr[t, rows_n + 1] = fhalo_r[1, t].astype(F32) * has_down
         frame_cols(t, 0)
         frame_cols(t, rows_n + 1)
+    gather_step(1)
+    gather_step(0)
+    small_next(0)
+    gather_step(2)
     for t in range(min(2, frames_n)):
         frame_pixels(t, 0, 1)
         frame_pixels(t, rows_n - 1, rows_n)
-    gather_step(1)
+    gather_step(3)
     if frames_n > 2:
         frame_pixels(2, 0, rows_n)
-    gather_step(2)
     gather_step(0)
     small_next(0)
-    gather_step(3)
     for t in range(3, frames_n):
         frame_pixels(t, 0, rows_n)
     gather_step(0)
@@ -412,18 +419,20 @@
             c.start()
             hid_copies.append(c)
 
-    order = list(range(1, nchunk - 1)) + [0, nchunk - 1]
-    slots = [(0, m) for m in range(nchunk)] + [(t, m) for t in range(1, frames_n) for m in order]
+    inner = list(range(1, nchunk - 1))
+    order = [inner + [nchunk - 1, 0], inner[::-1] + [0, nchunk - 1]]
+    slots = [(0, m) for m in range(nchunk)] + [(t, m) for t in range(1, frames_n) for m in order[(t + 1) % 2]]
     last_of = {t: [s for s in slots if s[0] == t][-1] for t in range(frames_n)}
     for i, (t, m) in enumerate(slots + [(frames_n, 0)]):
-        if t == 1 and m == order[0]:
+        if t == 1 and m == order[0][0]:
             for k in range(1, 4):
                 while steps[k] < 4:
                     gather_step(k)
-        if 0 < t < frames_n and m == order[nchunk - 2]:
-            for k in range(2):
-                halos[t - 1][k].wait_recv()
+        if 0 < t < frames_n and m == 0:
+            halos[t - 1][0].wait_recv()
             place_state(t - 1, shalo_r[t - 1, 0].astype(F32) * has_up, 0)
+        if 0 < t < frames_n and m == nchunk - 1:
+            halos[t - 1][1].wait_recv()
             place_state(t - 1, shalo_r[t - 1, 1].astype(F32) * has_down, rows_n + 1)
         if t < frames_n:
             forward_dot(t, m)
@@ -504,7 +513,7 @@
             gs[t % 2, at] = gs[t % 2, at] + row[k] if at in done else row[k]
             done.add(at)
 
-    work = [(t, m) for t in reversed(range(frames_n)) for m in order]
+    work = [(t, m) for t in reversed(range(frames_n)) for m in order[(frames_n - 1 - t) % 2]]
     backward_rows(*work[0])
     ghalos = [[None, None] for _ in range(frames_n)]
 
@@ -527,14 +536,14 @@
             ghalos[t][0] = remote(ghalo_s.at[t - 1, 1], ghalo_r.at[t - 1, 0], at_b, down_r)
     left = work[-(nchunk - 1) :]
 
-    stage = [0] * 3
-    flight = [None] * 3
-    parts = [[acc[q][0], acc[q][1] if ncore > 1 else acc[q][0].at[:, :, 0]] for q in range(3)]
-
+    stage = [0] * 4
+    flight = [None] * 4
+    last = len(PARTS) - 1
     def reduce_step(q):
         s = stage[q]
         stage[q] = s + 1
-        first, second = parts[q]
+        first = acc[q][0]
+        second = acc[q][1] if ncore > 1 else first.at[:, :, 0]
         if s == 0 and ncore > 1:
             core_send[q][...] = first[:, :, 1 - core].astype(BF16)
             flight[q] = [remote(core_send[q], core_recv[q], *core_peer(1))]
@@ -543,11 +552,18 @@
                 flight[q][0].wait_recv()
                 second[...] = first[:, :, core] + core_recv[q][...].astype(F32)
             flight[q] = []
+            if q >= DIRECT:
+                tail_send[q - DIRECT][...] = second[...].astype(BF16)
+                for k in range(1, nfar * nmid):
+                    to = lax.rem(far * nmid + mid + k, nfar * nmid)
+                    src = tail_send[q - DIRECT].at[to // nmid, to % nmid]
+                    flight[q].append(remote(src, tail_recv[q - DIRECT].at[k - 1], *device(to // nmid, to % nmid, core, low)))
+                return
             for k in range(1, nmid):
                 to = lax.rem(mid + k, nmid)
                 mid_send[q][k - 1] = second[:, to].astype(BF16)
                 flight[q].append(remote(mid_send[q].at[k - 1], mid_recv[q].at[k - 1], *mid_peer(k)))
-        elif s == 2:
+        elif s == 2 and q < DIRECT:
             total = second[:, mid]
             for k in range(1, nmid):
                 flight[q][k - 1].wait_recv()
@@ -558,87 +574,87 @@
             for k in range(1, nfar):
                 to = lax.rem(far + k, nfar)
                 flight[q].append(remote(far_send[q].at[to], far_recv[q].at[k - 1], *far_peer(k)))
-        elif s == 3:
+        elif s == 3 or s == 2:
+            stage[q] = 4
             total = second[far, mid]
-            for k in range(1, nfar):
-                flight[q][k - 1].wait_recv()
-                total = total + far_recv[q][k - 1].astype(F32)
+            arrived = tail_recv[q - DIRECT] if q >= DIRECT else far_recv[q]
+            for k in range(len(flight[q])):
+                flight[q][k].wait_recv()
+                total = total + arrived[k].astype(F32)
+            a, lo, up, _ = PARTS[q]
             for j in range(3):
-                at = (3 * q + j) * (CIN + HID)
-                nat[:, at : at + CIN] = total[:, WIDE + j * CIN : WIDE + (j + 1) * CIN]
-                nat[:, at + CIN : at + CIN + HID] = total[:, j * HID : (j + 1) * HID]
-
-    def kernel_dot(a, t):
-        return mm(xt[t - 1, :, a * WID : a * WID + pix], gpre[t], NN)
+                at = (3 * a + j) * (CIN + HID)
+                if up > WIDE:
+                    nat[:, at : at + CIN] = total[:, WIDE - lo + j * CIN : WIDE - lo + (j + 1) * CIN]
+                if lo <= j * HID < up:
+                    nat[:, at + CIN : at + CIN + HID] = total[:, j * HID - lo : (j + 1) * HID - lo]
+
+    def kernel_dot(q, t):
+        a, lo, up, _ = PARTS[q]
+        return mm(xt[t - 1, lo:up, a * WID : a * WID + pix], gpre[t], NN)
 
     def finish_rows(k):
         rows_ready(*left[k])
         backward_rows(*left[k])
 
-    def place_chunk(a, total):
-        extra = total[WIDE:, :] + fzero[a * FEAT : (a + 1) * FEAT, :]
-        whole = jnp.concatenate([total[:WIDE, :], extra, jnp.zeros((PART - WIDE - FEAT, GATES), F32)], axis=0)
-        acc[a][0][...] = whole.T.reshape(acc[a][0].shape)
-
-    totals = [None] * 3
-    for a in range(3):
+    def place_part(q, total):
+        a, lo, up, wide = PARTS[q]
+        pieces = [total]
+        if up > WIDE:
+            pieces = [total[: WIDE - lo], total[WIDE - lo :] + fzero[a * FEAT : (a + 1) * FEAT, :]]
+        if wide > up - lo:
+            pieces.append(jnp.zeros((wide - up + lo, GATES), F32))
+        acc[q][0][...] = jnp.concatenate(pieces, axis=0).T.reshape(acc[q][0].shape)
+
+    after = {(1, 1): [0], (1, 2): [0], (2, 1): [1], (2, 2): [1], (3, 1): [2], (3, 2): [2]}
+    totals = [None] * 4
+    for q in range(4):
         for t in range(1, frames_n):
-            part = kernel_dot(a, t)
-            totals[a] = part if t == 1 else totals[a] + part
-            if a == 0 and t - 1 < len(left):
+            part = kernel_dot(q, t)
+            totals[q] = part if t == 1 else totals[q] + part
+            if q == 0 and t - 1 < len(left):
                 finish_rows(t - 1)
-            if a > 0 and t == 1:
-                place_chunk(a - 1, totals[a - 1])
-                reduce_step(a - 1)
-            if a > 0 and t == 2:
-                if a > 1:
-                    reduce_step(a - 2)
-                reduce_step(a - 1)
-                small_next(1)
-        if a == 0:
+            if q > 0 and t == 1:
+                place_part(q - 1, totals[q - 1])
+            for k in after.get((q, t), []):
+                reduce_step(k)
+        if q == 0:
             for k in range(frames_n - 1, len(left)):
                 finish_rows(k)
             g0 = [xt0[:, k * WID : k * WID + pix] for k in range(3)]
             fzero[...] = mm(jnp.concatenate(g0, axis=0), gpre[0], NN)
             rows = [jnp.sum(sums[i], axis=0, keepdims=True) for i in range(7)]
             small_next(1, jnp.concatenate(rows[4:] + [jnp.zeros((1, HID), F32)] + rows[:4], axis=0))
-    place_chunk(2, totals[2])
-    reduce_step(2)
+        elif q < 3:
+            small_next(1)
+    place_part(last, totals[last])
+    reduce_step(last)
+    reduce_step(0)
 
     fgb = fr
 
     def frame_back(t):
-        fgb[t] = jnp.zeros(fgb.shape[1:], F32)
-
-        def chunk(m, carry):
-            px = pl.ds(pl.multiple_of(m * CH * WID, CH * WID), CH * WID)
-            y = mm(wft[0 : 9 * CIN, :], gpre[t, px, :], NT)
-            for i in range(CH):
-                for a in range(3):
-                    part = y[a * FEAT : (a + 1) * FEAT, i * WID : (i + 1) * WID]
-                    z = part[CIN : 2 * CIN]
-                    z = z + lane_shift(part[0:CIN], 1)
-                    z = z + lane_shift(part[2 * CIN :], -1)
-                    at = m * CH + i + a
-                    fgb[t, at] = fgb[t, at] + z
-            return carry
-
-        lax.fori_loop(0, nchunk, chunk, 0)
-        bhalo_s[0, t] = fgb[t, 0].astype(BF16)
-        bhalo_s[1, t] = fgb[t, rows_n + 1].astype(BF16)
+        y = mm(wft[0 : 9 * CIN, :], gpre[t], NT)
+        row = [None] * (rows_n + 2)
+        for i in range(rows_n):
+            for a in range(3):
+                part = y[a * FEAT : (a + 1) * FEAT, i * WID : (i + 1) * WID]
+                z = part[CIN : 2 * CIN] + lane_shift(part[0:CIN], 1) + lane_shift(part[2 * CIN :], -1)
+                row[i + a] = z if row[i + a] is None else row[i + a] + z
+        for at in range(rows_n + 2):
+            fgb[t, at] = row[at]
+        bhalo_s[0, t] = row[0].astype(BF16)
+        bhalo_s[1, t] = row[rows_n + 1].astype(BF16)
 
     wft[...] = cat_wt(HALL, KALL).astype(F32).T.astype(BF16)
-    after = [[2], [1, 0], [], []]
+    between = [[last], [], [1], [2]]
     for t in range(frames_n):
         frame_back(t)
-        for q in after[t] if t < 4 else []:
+        for q in between[t] if t < 4 else []:
             reduce_step(q)
     f_up = remote(bhalo_s.at[0], bhalo_r.at[1], at_b, up_r)
     f_down = remote(bhalo_s.at[1], bhalo_r.at[0], at_b, down_r)
-    for q in (2, 1, 0):
-        while stage[q] < 3:
-            reduce_step(q)
-    for q in range(3):
+    for q in (0, 3, 1, 2):
         while stage[q] < 4:
             reduce_step(q)
     if nlow > 1:
@@ -775,15 +791,15 @@
     bias_row = gate_bias.reshape(1, own)
 
     vm = pltpu.VMEM
-    part = (UNIT, PART)
     pair = (nfar, nmid) if ncore > 1 else (1, 1)
-    acc_shapes = [
-        [vm((nfar, nmid, ncore) + part, F32), vm(pair + part, F32)] for _ in range(3)
-    ]
+    wides = [(UNIT, part[3]) for part in PARTS]
+    acc_shapes = [[vm((nfar, nmid, ncore) + wide, F32), vm(pair + wide, F32)] for wide in wides]
     ncopies = (
         2 * (nfar + nmid + ncore + nlow - 4)
         + 4 * (nfar + nmid + ncore - 3)
-        + 3 * (nfar + nmid + ncore - 3)
+        + DIRECT * (nfar + nmid - 2)
+        + len(PARTS) * (ncore - 1)
+        + (len(PARTS) - DIRECT) * (nfar * nmid - 1)
         + 4
         + 4 * (frames_n - 1)
         + 2 * (nlow - 1)
@@ -814,10 +830,15 @@
         vm((2, frames_n, CIN, WID), BF16),
         vm((UNIT, KALL), F32),
     ]
-    scratch += [vm(pair + part, BF16)] * 6
-    scratch += [vm((nmid - 1, nfar) + part, BF16)] * 6
-    scratch += [vm((nfar,) + part, BF16)] * 3 + [vm((nfar - 1,) + part, BF16)] * 3
+    scratch += [vm(pair + wide, BF16) for wide in wides + wides]
+    two = [wide if q < DIRECT else (8, HID) for q, wide in enumerate(wides)]
+    mids = [(nmid - 1, nfar) if q < DIRECT else (1, 1) for q in range(len(two))]
+    fars = [(nfar,) if q < DIRECT else (1,) for q in range(len(two))]
+    scratch += [vm(mids[q] + two[q], BF16) for q in range(len(two))] * 2
+    scratch += [vm(fars[q] + two[q], BF16) for q in range(len(two))] * 2
     scratch += [vm((2, size, 8, HID), F32) for size in (nfar, nmid, ncore, nlow)]
+    scratch += [vm((nfar, nmid) + wide, BF16) for wide in wides[DIRECT:]]
+    scratch += [vm((nfar * nmid - 1,) + wide, BF16) for wide in wides[DIRECT:]]
     scratch += [vm((UNIT, KALL), BF16), vm((2, max(1, nlow - 1), UNIT, KALL), BF16)]
     scratch += [vm((nbat * nrow, 8, HID), F32), pltpu.SemaphoreType.DMA((2, nbat * nrow))]
     scratch += [

time: 88.6 us -> 85.2 us (0.962)
  Pallas kernels: 87.5 us -> 84.2 us
    pallas_call x1, Pallas kernels: 83 us -> 79.7 us  [local(): pl.pallas_call(functools.partial(layer_kernel, dims), out_shape=(jax.Shap...]
where the time goes in v4:
time: 85.2 us; the launch traced here: 85 us
  Pallas kernels  84.2 us (99%)
    pallas_call x1, Pallas kernels, local(): pl.pallas_call(functools.partial(layer_kernel, dims), out_shape=(jax.Shap...  79.7 us
    pallas_call x1, Pallas kernels, local(): pl.pallas_call(functools.partial(update_kernel, (nbat, nrow)), out_shape=...  4.52 us

profile of v4, /device:TPU:0, one launch (start us, length us, event | category | flops | bytes accessed | tf_op | source)
XLA Modules:
  0.0 85.0 jit_solution(5823545789855714800)
XLA Ops:
  0.6 79.7 %layer.1 = (bf16[1,4,16,128,128]{4,3,2,1,0:T(8,128)(2,1)}, f32[1,4,16,16,128]{4,3,2,1,0:T(8,128)}, f32[16,1296]{1,0:T(8,128)}, f32[8,128]{1,0:T(8,128)}, f32[8,128]{1,0:T(8,128)}) custom-call(s32[1,2]{1,0:T(1,128)} %crop_ref.1, bf16[1,4,16,16,128]{4,3,2,1,0:T(8,128)(2,1)} %frames_ref.1, f32[16,1296]{1,0:T(8,128)} %bitcast.13, f32[1,16]{1,0:T(1,128)} %bitcast.17, ...), custom_call_target="tpu_custom_call" | custom-call | tf_op jit(solution)/shard_map/layer/pallas_call | solution.py:853
  80.3 4.5 %update.1 = (bf16[1,4,16,128,128]{4,3,2,1,0:T(8,128)(2,1)}, f32[1,4,16,16,128]{4,3,2,1,0:T(8,128)}, f32[1,1]{1,0:T(1,128)}, f32[16,1296]{1,0:T(8,128)}, f32[16,1...) custom-call(bf16[1,4,16,128,128]{4,3,2,1,0:T(8,128)(2,1)} %get-tuple, ...), custom_call_target="tpu_custom_call" | custom-call | tf_op jit(solution)/shard_map/update/pallas_call | solution.py:876

commit v5 on v4

--- a/solution.py
+++ b/solution.py
@@ -694,15 +694,14 @@
     c = pltpu.make_async_copy(fgo, fg_hbm.at[0], lsems.at[1 + frames_n])
     c.start()
     hid_copies.append(c)
+    for c in pending:
+        c.wait_send()
+    for c in hid_copies:
+        c.wait()
     lax.fori_loop(1, ndev, lambda k, c: (norm_copy(k).wait_recv(), c)[1], 0)
     squares = jnp.sum(norm_tiles[:, 0:1, :], axis=0) + jnp.sum(small * small)
     norm_out[...] = jnp.broadcast_to(jnp.sqrt(squares), (8, HID))
     lax.fori_loop(1, ndev, lambda k, c: (norm_copy(k).wait_send(), c)[1], 0)
-
-    for c in hid_copies:
-        c.wait()
-    for c in pending:
-        c.wait_send()
 
 
 def adamw_update(weight, gradient, first, second, scale):

time: 85.2 us -> 85.1 us (level)
  no operation moved by 1% of the time
where the time goes in v5:
time: 85.1 us; the launch traced here: 84.9 us
  Pallas kernels  84 us (99%)
    pallas_call x1, Pallas kernels, local(): pl.pallas_call(functools.partial(layer_kernel, dims), out_shape=(jax.Shap...  79.5 us
    pallas_call x1, Pallas kernels, local(): pl.pallas_call(functools.partial(update_kernel, (nbat, nrow)), out_shape=...  4.52 us

profile of v5, /device:TPU:0, one launch (start us, length us, event | category | flops | bytes accessed | tf_op | source)
XLA Modules:
  0.0 84.9 jit_solution(13756227046487033064)
XLA Ops:
  0.6 79.5 %layer.1 = (bf16[1,4,16,128,128]{4,3,2,1,0:T(8,128)(2,1)}, f32[1,4,16,16,128]{4,3,2,1,0:T(8,128)}, f32[16,1296]{1,0:T(8,128)}, f32[8,128]{1,0:T(8,128)}, f32[8,128]{1,0:T(8,128)}) custom-call(s32[1,2]{1,0:T(1,128)} %crop_ref.1, bf16[1,4,16,16,128]{4,3,2,1,0:T(8,128)(2,1)} %frames_ref.1, f32[16,1296]{1,0:T(8,128)} %bitcast.13, f32[1,16]{1,0:T(1,128)} %bitcast.17, ...), custom_call_target="tpu_custom_call" | custom-call | tf_op jit(solution)/shard_map/layer/pallas_call | solution.py:852
  80.2 4.5 %update.1 = (bf16[1,4,16,128,128]{4,3,2,1,0:T(8,128)(2,1)}, f32[1,4,16,16,128]{4,3,2,1,0:T(8,128)}, f32[1,1]{1,0:T(1,128)}, f32[16,1296]{1,0:T(8,128)}, f32[16,1...) custom-call(bf16[1,4,16,128,128]{4,3,2,1,0:T(8,128)(2,1)} %get-tuple, ...), custom_call_target="tpu_custom_call" | custom-call | tf_op jit(solution)/shard_map/update/pallas_call | solution.py:875
